TPU v7x, 32 devices: a whole 2x2x4 slice. The times are simulated.
32 devices in a mesh: groups: 2 (over x), blk: 16 (over z, y, core).
Axes of the slice: x: 2, y: 2, z: 4, core: 2. Of those that a mesh axis runs over, the one named last changes fastest.
Arguments:
- queries: bfloat16 [4096, 512], P(('groups', 'blk')), parts along dimension 0, may hold values from -8 to 8
- key_states: bfloat16 [4096, 128], P(('groups', 'blk')), parts along dimension 0, may hold values from -6 to 6
- value_states: bfloat16 [4096, 128], P(('groups', 'blk')), parts along dimension 0, may hold values from -6 to 6
- grad_out: bfloat16 [4096, 512], P(('groups', 'blk')), parts along dimension 0, may hold values from -6 to 6
- tile_mask: int32 [32, 16], P('groups'), parts along dimension 0, may hold values 0 or 1
- block_order: int32 [32], P('groups'), parts along dimension 0, may hold values from 0 to 15, each once
Outputs:
- attended: bfloat16 [4096, 512], P(('groups', 'blk')), parts along dimension 0
- grad_queries: bfloat16 [4096, 512], P(('groups', 'blk')), parts along dimension 0
- grad_keys: float32 [4096, 128], P(('groups', 'blk')), parts along dimension 0
- grad_values: float32 [4096, 128], P(('groups', 'blk')), parts along dimension 0
There are 2 independent parts, one for each index of `groups`. A program takes and returns all parts, laid end to end along the dimension named above; each array names one. Nothing has to cross between parts.
Inputs may be any that keep to these rules, and one draw needn't show every extreme that they name: `block_order`: each block number appears once.
All inputs are finite; a program needn't handle non-finite values.
Results may differ from a plain program's by a relative error of at most 0.04.
Values may be sent and summed in bfloat16 or wider, within the bound.
A program may use at most 64 MiB of HBM per device.

v0:
```python
import jax
import jax.numpy as jnp
from jax import lax
from jax.sharding import PartitionSpec as P

TILE = 128


def passed_along(value, axis, steps):
    count = lax.axis_size(axis)
    pairs = [(source, (source + steps) % count) for source in range(count)]
    return lax.ppermute(value, axis, pairs)


def shards(queries, key_states, value_states, grad_out, tile_mask, block_order):
    cycle_size = lax.axis_size("blk")
    my_index = lax.axis_index("blk")
    tok_rows = key_states.shape[0]
    head_width = key_states.shape[1]
    head_count = queries.shape[1] // head_width
    scaling = head_width ** (-0.5)
    tiles_per = tok_rows // TILE
    tile_total = tile_mask.shape[1]
    offsets = jnp.arange(tok_rows, dtype=jnp.int32)
    my_block = block_order[my_index]
    total_rows = head_count * tok_rows

    def to_rows(features):
        return (
            features.reshape(tok_rows, head_count, head_width)
            .transpose(1, 0, 2)
            .reshape(total_rows, head_width)
        )

    def from_rows(row_form):
        return (
            row_form.reshape(head_count, tok_rows, head_width)
            .transpose(1, 0, 2)
            .reshape(tok_rows, head_count * head_width)
        )

    query_rows = to_rows(queries)
    cot_rows = to_rows(grad_out)

    def mask_for(query_block, key_pos):
        query_pos = query_block * tok_rows + offsets
        tile_rows = lax.dynamic_slice_in_dim(
            tile_mask, query_block * tiles_per, tiles_per, 0
        ).astype(jnp.float32)
        tile_rows = jnp.repeat(tile_rows, TILE, axis=0)
        one_hot = (
            (key_pos // TILE)[:, None] == jnp.arange(tile_total, dtype=jnp.int32)[None, :]
        ).astype(jnp.float32)
        tile_bits = jnp.dot(tile_rows, one_hot.T, preferred_element_type=jnp.float32) > 0.5
        same_tile = (query_pos // TILE)[:, None] == (key_pos // TILE)[None, :]
        allowed = (query_pos[:, None] >= key_pos[None, :]) & (tile_bits | same_tile)
        return jnp.tile(allowed, (head_count, 1))

    def softmax_update(carry_state, key_sub, value_sub, allowed):
        run_max, run_sum, run_acc = carry_state
        scores = (
            jnp.einsum("rd,kd->rk", query_rows, key_sub, preferred_element_type=jnp.float32)
            * scaling
        )
        scores = jnp.where(allowed, scores, -1e30)
        new_max = jnp.maximum(run_max, jnp.max(scores, axis=1))
        weights = jnp.where(allowed, jnp.exp(scores - new_max[:, None]), 0.0)
        factor = jnp.exp(run_max - new_max)
        run_sum = run_sum * factor + jnp.sum(weights, axis=1)
        run_acc = run_acc * factor[:, None] + jnp.dot(
            weights.astype(jnp.bfloat16), value_sub, preferred_element_type=jnp.float32
        )
        return (new_max, run_sum, run_acc)

    def guarded_update(carry_state, key_sub, value_sub, allowed):
        return softmax_update(carry_state, key_sub, value_sub, allowed)

    start_state = (
        jnp.full((total_rows,), -1e30, jnp.float32),
        jnp.zeros((total_rows,), jnp.float32),
        jnp.zeros((total_rows, head_width), jnp.float32),
    )
    key_piece = lax.all_gather(key_states, "blk", axis=0, tiled=True)
    value_piece = lax.all_gather(value_states, "blk", axis=0, tiled=True)
    piece_rows = key_piece.shape[0]

    def sub_step(sub_num, inner_state):
        first = sub_num * tok_rows
        key_sub = lax.dynamic_slice_in_dim(key_piece, first, tok_rows, 0)
        value_sub = lax.dynamic_slice_in_dim(value_piece, first, tok_rows, 0)
        key_ids = first + jnp.arange(tok_rows, dtype=jnp.int32)
        owners = key_ids // tok_rows
        owner_blocks = jnp.sum(
            jnp.where(
                owners[:, None] == jnp.arange(cycle_size, dtype=jnp.int32)[None, :],
                block_order[None, :],
                0,
            ),
            axis=1,
        )
        key_pos = owner_blocks * tok_rows + key_ids % tok_rows
        return guarded_update(inner_state, key_sub, value_sub, mask_for(my_block, key_pos))

    run_max, run_sum, run_acc = lax.fori_loop(0, piece_rows // tok_rows, sub_step, start_state)
    log_sum = run_max + jnp.log(run_sum)
    out_rows = (run_acc / run_sum[:, None]).astype(jnp.bfloat16)
    attended = from_rows(out_rows)
    row_delta = jnp.sum(cot_rows.astype(jnp.float32) * out_rows.astype(jnp.float32), axis=1)

    def block_grads(q_part, cot_part, sum_part, delta_part, key_sub, value_sub, allowed):
        scores = (
            jnp.einsum("rd,kd->rk", q_part, key_sub, preferred_element_type=jnp.float32) * scaling
        )
        weights = jnp.where(allowed, jnp.exp(scores - sum_part[:, None]), 0.0)
        value_term = jnp.einsum(
            "rk,rd->kd", weights.astype(jnp.bfloat16), cot_part, preferred_element_type=jnp.float32
        )
        d_prob = jnp.einsum("rd,kd->rk", cot_part, value_sub, preferred_element_type=jnp.float32)
        d_score = (weights * (d_prob - delta_part[:, None])).astype(jnp.bfloat16)
        query_term = jnp.dot(d_score, key_sub, preferred_element_type=jnp.float32) * scaling
        key_term = (
            jnp.einsum("rk,rd->kd", d_score, q_part, preferred_element_type=jnp.float32) * scaling
        )
        return (query_term, key_term, value_term)

    def guarded_grads(q_part, cot_part, sum_part, delta_part, key_sub, value_sub, allowed):
        return block_grads(q_part, cot_part, sum_part, delta_part, key_sub, value_sub, allowed)

    zero_keys = jnp.zeros((tok_rows, head_width), jnp.float32)
    zero_queries = jnp.zeros((total_rows, head_width), jnp.float32)

    def key_step(step_num, carry_state):
        key_cur, value_cur, key_acc, value_acc, query_acc = carry_state
        source = (my_index - step_num) % cycle_size
        key_pos = block_order[source] * tok_rows + offsets
        allowed = mask_for(my_block, key_pos)
        query_term, key_term, value_term = guarded_grads(
            query_rows, cot_rows, log_sum, row_delta, key_cur, value_cur, allowed
        )
        return (
            key_cur,
            value_cur,
            key_acc + key_term,
            value_acc + value_term,
            query_acc + query_term,
        )

    def key_turn(step_num, carry_state):
        key_cur, value_cur, key_acc, value_acc, query_acc = key_step(step_num, carry_state)
        key_cur, value_cur = passed_along((key_cur, value_cur), "blk", 1)
        key_acc, value_acc = passed_along((key_acc, value_acc), "blk", 1)
        return (key_cur, value_cur, key_acc, value_acc, query_acc)

    carry_state = (key_states, value_states, zero_keys, zero_keys, zero_queries)
    carry_state = lax.fori_loop(0, cycle_size - 1, key_turn, carry_state)
    carry_state = key_step(cycle_size - 1, carry_state)
    key_acc, value_acc = passed_along((carry_state[2], carry_state[3]), "blk", 1)
    query_acc = carry_state[4]
    grad_queries = from_rows(query_acc.astype(jnp.bfloat16))
    return (attended, grad_queries, key_acc, value_acc)


def solution(mesh):
    placed = (
        P(("groups", "blk"), None),
        P(("groups", "blk"), None),
        P(("groups", "blk"), None),
        P(("groups", "blk"), None),
        P("groups", None),
        P("groups"),
    )
    return jax.shard_map(
        shards,
        mesh=mesh,
        in_specs=placed,
        out_specs=(
            P(("groups", "blk"), None),
            P(("groups", "blk"), None),
            P(("groups", "blk"), None),
            P(("groups", "blk"), None),
        ),
        check_vma=False,
    )
```

profile of v0, /device:TPU:0, one launch (start us, length us, event | category | flops | bytes accessed | tf_op | source)
XLA Modules:
  0.0 222.9 jit_solution(3966216597943441637)
XLA Ops:
  0.7 0.8 copy.83
  6.8 24.6 %all_gather.6 = bf16[2048,128]{1,0:T(8,128)(2,1)S(1)} all-gather(bf16[128,128]{1,0:T(8,128)(2,1)S(1)} %copy.83), channel_id=1, replica_groups=mesh['groups'=2,'blk'=16] {'blk'}, dimensions={0}, use_global_device_ids=true | all-gather | bytes 557056 | tf_op jit(solution)/shard_map/all_gather | solution.py:83
  31.4 18.9 %all_gather.7 = bf16[2048,128]{1,0:T(8,128)(2,1)S(1)} all-gather(bf16[128,128]{1,0:T(8,128)(2,1)S(1)} %copy.84), channel_id=1, replica_groups=mesh['groups'=2,'blk'=16] {'blk'}, dimensions={0}, use_global_device_ids=true | all-gather | bytes 557056 | tf_op jit(solution)/shard_map/all_gather | solution.py:84
  50.2 17.7 %while.47 = (s32[]{:T(128)}, f32[512]{0:T(512)S(1)}, f32[512]{0:T(512)S(1)}, f32[512,128]{1,0:T(8,128)S(1)}, s32[]{:T(128)}, /*index=5*/s32[16]{0:T(128)S(1)}, b...) while((s32[]{:T(128)}, f32[512]{0:T(512)S(1)}, ...), condition=%wide.region_4.5_spmd.clone, body=%wide.region_0.4_spmd.clone.sunk | while | flops 34965508 | bytes 1841459 | solution.py:104
  69.2 144.8 %while.48 = (s32[]{:T(128)}, bf16[128,128]{1,0:T(8,128)(2,1)S(1)}, bf16[128,128]{1,0:T(8,128)(2,1)S(1)}, f32[128,128]{1,0:T(8,128)S(1)}, f32[128,128]{1,0:T(8,12...) while((s32[]{:T(128)}, bf16[128,128]{1,0:T(8,128)(2,1)S(1)}, ...), condition=%wide.region_7.8_spmd.clone.clone, body=%wide.region_6.7_spmd.clone.clone.sunk | while | flops 85202960 | bytes 3711538 | solution.py:155
  69.7 1.5 collective-permute-start.1
  74.4 0.9 collective-permute-done
  75.7 4.2 %collective-permute-done.2 = f32[128,128]{1,0:T(8,128)S(1)} collective-permute-done((f32[128,128]{1,0:T(8,128)S(1)}, f32[128,128]{1,0:T(8,128)S(1)}, u32[]{:S(2)}, u32[]{:S(2)}) %collective-permute-start.2) | collective-permute-done | bytes 65568 | tf_op jit(solution)/shard_map/while/body/eval_jaxpr/ppermute | solution.py:12
  79.9 0.7 collective-permute-done.3
  83.6 3.1 %collective-permute-done = bf16[128,128]{1,0:T(8,128)(2,1)S(1)} collective-permute-done((bf16[128,128]{1,0:T(8,128)(2,1)S(1)}, bf16[128,128]{1,0:T(8,128)(2,1)S(1)}, u32[]{:S(2)}, u32[]{:S(2)}) %collective-permute-start) | collective-permute-done | bytes 32800 | tf_op jit(solution)/shard_map/while/body/eval_jaxpr/ppermute | solution.py:12
  87.0 2.4 %collective-permute-done.2 = f32[128,128]{1,0:T(8,128)S(1)} collective-permute-done((f32[128,128]{1,0:T(8,128)S(1)}, f32[128,128]{1,0:T(8,128)S(1)}, u32[]{:S(2)}, u32[]{:S(2)}) %collective-permute-start.2) | collective-permute-done | bytes 65568 | tf_op jit(solution)/shard_map/while/body/eval_jaxpr/ppermute | solution.py:12
  89.4 0.7 collective-permute-done.3
  93.1 3.1 %collective-permute-done = bf16[128,128]{1,0:T(8,128)(2,1)S(1)} collective-permute-done((bf16[128,128]{1,0:T(8,128)(2,1)S(1)}, bf16[128,128]{1,0:T(8,128)(2,1)S(1)}, u32[]{:S(2)}, u32[]{:S(2)}) %collective-permute-start) | collective-permute-done | bytes 32800 | tf_op jit(solution)/shard_map/while/body/eval_jaxpr/ppermute | solution.py:12
  96.5 2.4 %collective-permute-done.2 = f32[128,128]{1,0:T(8,128)S(1)} collective-permute-done((f32[128,128]{1,0:T(8,128)S(1)}, f32[128,128]{1,0:T(8,128)S(1)}, u32[]{:S(2)}, u32[]{:S(2)}) %collective-permute-start.2) | collective-permute-done | bytes 65568 | tf_op jit(solution)/shard_map/while/body/eval_jaxpr/ppermute | solution.py:12
  98.9 0.7 collective-permute-done.3
  102.6 3.1 %collective-permute-done = bf16[128,128]{1,0:T(8,128)(2,1)S(1)} collective-permute-done((bf16[128,128]{1,0:T(8,128)(2,1)S(1)}, bf16[128,128]{1,0:T(8,128)(2,1)S(1)}, u32[]{:S(2)}, u32[]{:S(2)}) %collective-permute-start) | collective-permute-done | bytes 32800 | tf_op jit(solution)/shard_map/while/body/eval_jaxpr/ppermute | solution.py:12
  106.0 2.4 %collective-permute-done.2 = f32[128,128]{1,0:T(8,128)S(1)} collective-permute-done((f32[128,128]{1,0:T(8,128)S(1)}, f32[128,128]{1,0:T(8,128)S(1)}, u32[]{:S(2)}, u32[]{:S(2)}) %collective-permute-start.2) | collective-permute-done | bytes 65568 | tf_op jit(solution)/shard_map/while/body/eval_jaxpr/ppermute | solution.py:12
  108.5 0.7 collective-permute-done.3
  112.2 3.1 %collective-permute-done = bf16[128,128]{1,0:T(8,128)(2,1)S(1)} collective-permute-done((bf16[128,128]{1,0:T(8,128)(2,1)S(1)}, bf16[128,128]{1,0:T(8,128)(2,1)S(1)}, u32[]{:S(2)}, u32[]{:S(2)}) %collective-permute-start) | collective-permute-done | bytes 32800 | tf_op jit(solution)/shard_map/while/body/eval_jaxpr/ppermute | solution.py:12
  115.6 2.4 %collective-permute-done.2 = f32[128,128]{1,0:T(8,128)S(1)} collective-permute-done((f32[128,128]{1,0:T(8,128)S(1)}, f32[128,128]{1,0:T(8,128)S(1)}, u32[]{:S(2)}, u32[]{:S(2)}) %collective-permute-start.2) | collective-permute-done | bytes 65568 | tf_op jit(solution)/shard_map/while/body/eval_jaxpr/ppermute | solution.py:12
  118.0 0.7 collective-permute-done.3
  121.7 3.1 %collective-permute-done = bf16[128,128]{1,0:T(8,128)(2,1)S(1)} collective-permute-done((bf16[128,128]{1,0:T(8,128)(2,1)S(1)}, bf16[128,128]{1,0:T(8,128)(2,1)S(1)}, u32[]{:S(2)}, u32[]{:S(2)}) %collective-permute-start) | collective-permute-done | bytes 32800 | tf_op jit(solution)/shard_map/while/body/eval_jaxpr/ppermute | solution.py:12
  125.1 2.4 %collective-permute-done.2 = f32[128,128]{1,0:T(8,128)S(1)} collective-permute-done((f32[128,128]{1,0:T(8,128)S(1)}, f32[128,128]{1,0:T(8,128)S(1)}, u32[]{:S(2)}, u32[]{:S(2)}) %collective-permute-start.2) | collective-permute-done | bytes 65568 | tf_op jit(solution)/shard_map/while/body/eval_jaxpr/ppermute | solution.py:12
  127.5 0.7 collective-permute-done.3
  131.2 3.1 %collective-permute-done = bf16[128,128]{1,0:T(8,128)(2,1)S(1)} collective-permute-done((bf16[128,128]{1,0:T(8,128)(2,1)S(1)}, bf16[128,128]{1,0:T(8,128)(2,1)S(1)}, u32[]{:S(2)}, u32[]{:S(2)}) %collective-permute-start) | collective-permute-done | bytes 32800 | tf_op jit(solution)/shard_map/while/body/eval_jaxpr/ppermute | solution.py:12
  134.6 2.4 %collective-permute-done.2 = f32[128,128]{1,0:T(8,128)S(1)} collective-permute-done((f32[128,128]{1,0:T(8,128)S(1)}, f32[128,128]{1,0:T(8,128)S(1)}, u32[]{:S(2)}, u32[]{:S(2)}) %collective-permute-start.2) | collective-permute-done | bytes 65568 | tf_op jit(solution)/shard_map/while/body/eval_jaxpr/ppermute | solution.py:12
  137.1 0.7 collective-permute-done.3
  140.8 3.1 %collective-permute-done = bf16[128,128]{1,0:T(8,128)(2,1)S(1)} collective-permute-done((bf16[128,128]{1,0:T(8,128)(2,1)S(1)}, bf16[128,128]{1,0:T(8,128)(2,1)S(1)}, u32[]{:S(2)}, u32[]{:S(2)}) %collective-permute-start) | collective-permute-done | bytes 32800 | tf_op jit(solution)/shard_map/while/body/eval_jaxpr/ppermute | solution.py:12
  144.2 2.4 %collective-permute-done.2 = f32[128,128]{1,0:T(8,128)S(1)} collective-permute-done((f32[128,128]{1,0:T(8,128)S(1)}, f32[128,128]{1,0:T(8,128)S(1)}, u32[]{:S(2)}, u32[]{:S(2)}) %collective-permute-start.2) | collective-permute-done | bytes 65568 | tf_op jit(solution)/shard_map/while/body/eval_jaxpr/ppermute | solution.py:12
  146.6 0.7 collective-permute-done.3
  150.3 3.1 %collective-permute-done = bf16[128,128]{1,0:T(8,128)(2,1)S(1)} collective-permute-done((bf16[128,128]{1,0:T(8,128)(2,1)S(1)}, bf16[128,128]{1,0:T(8,128)(2,1)S(1)}, u32[]{:S(2)}, u32[]{:S(2)}) %collective-permute-start) | collective-permute-done | bytes 32800 | tf_op jit(solution)/shard_map/while/body/eval_jaxpr/ppermute | solution.py:12
  153.7 2.4 %collective-permute-done.2 = f32[128,128]{1,0:T(8,128)S(1)} collective-permute-done((f32[128,128]{1,0:T(8,128)S(1)}, f32[128,128]{1,0:T(8,128)S(1)}, u32[]{:S(2)}, u32[]{:S(2)}) %collective-permute-start.2) | collective-permute-done | bytes 65568 | tf_op jit(solution)/shard_map/while/body/eval_jaxpr/ppermute | solution.py:12
  156.1 0.7 collective-permute-done.3
  159.8 3.1 %collective-permute-done = bf16[128,128]{1,0:T(8,128)(2,1)S(1)} collective-permute-done((bf16[128,128]{1,0:T(8,128)(2,1)S(1)}, bf16[128,128]{1,0:T(8,128)(2,1)S(1)}, u32[]{:S(2)}, u32[]{:S(2)}) %collective-permute-start) | collective-permute-done | bytes 32800 | tf_op jit(solution)/shard_map/while/body/eval_jaxpr/ppermute | solution.py:12
  163.2 2.4 %collective-permute-done.2 = f32[128,128]{1,0:T(8,128)S(1)} collective-permute-done((f32[128,128]{1,0:T(8,128)S(1)}, f32[128,128]{1,0:T(8,128)S(1)}, u32[]{:S(2)}, u32[]{:S(2)}) %collective-permute-start.2) | collective-permute-done | bytes 65568 | tf_op jit(solution)/shard_map/while/body/eval_jaxpr/ppermute | solution.py:12
  165.7 0.7 collective-permute-done.3
  169.4 3.1 %collective-permute-done = bf16[128,128]{1,0:T(8,128)(2,1)S(1)} collective-permute-done((bf16[128,128]{1,0:T(8,128)(2,1)S(1)}, bf16[128,128]{1,0:T(8,128)(2,1)S(1)}, u32[]{:S(2)}, u32[]{:S(2)}) %collective-permute-start) | collective-permute-done | bytes 32800 | tf_op jit(solution)/shard_map/while/body/eval_jaxpr/ppermute | solution.py:12
  172.8 2.4 %collective-permute-done.2 = f32[128,128]{1,0:T(8,128)S(1)} collective-permute-done((f32[128,128]{1,0:T(8,128)S(1)}, f32[128,128]{1,0:T(8,128)S(1)}, u32[]{:S(2)}, u32[]{:S(2)}) %collective-permute-start.2) | collective-permute-done | bytes 65568 | tf_op jit(solution)/shard_map/while/body/eval_jaxpr/ppermute | solution.py:12
  175.2 0.7 collective-permute-done.3
  178.9 3.1 %collective-permute-done = bf16[128,128]{1,0:T(8,128)(2,1)S(1)} collective-permute-done((bf16[128,128]{1,0:T(8,128)(2,1)S(1)}, bf16[128,128]{1,0:T(8,128)(2,1)S(1)}, u32[]{:S(2)}, u32[]{:S(2)}) %collective-permute-start) | collective-permute-done | bytes 32800 | tf_op jit(solution)/shard_map/while/body/eval_jaxpr/ppermute | solution.py:12
  182.3 2.4 %collective-permute-done.2 = f32[128,128]{1,0:T(8,128)S(1)} collective-permute-done((f32[128,128]{1,0:T(8,128)S(1)}, f32[128,128]{1,0:T(8,128)S(1)}, u32[]{:S(2)}, u32[]{:S(2)}) %collective-permute-start.2) | collective-permute-done | bytes 65568 | tf_op jit(solution)/shard_map/while/body/eval_jaxpr/ppermute | solution.py:12
  188.4 3.1 %collective-permute-done = bf16[128,128]{1,0:T(8,128)(2,1)S(1)} collective-permute-done((bf16[128,128]{1,0:T(8,128)(2,1)S(1)}, bf16[128,128]{1,0:T(8,128)(2,1)S(1)}, u32[]{:S(2)}, u32[]{:S(2)}) %collective-permute-start) | collective-permute-done | bytes 32800 | tf_op jit(solution)/shard_map/while/body/eval_jaxpr/ppermute | solution.py:12
  191.8 2.4 %collective-permute-done.2 = f32[128,128]{1,0:T(8,128)S(1)} collective-permute-done((f32[128,128]{1,0:T(8,128)S(1)}, f32[128,128]{1,0:T(8,128)S(1)}, u32[]{:S(2)}, u32[]{:S(2)}) %collective-permute-start.2) | collective-permute-done | bytes 65568 | tf_op jit(solution)/shard_map/while/body/eval_jaxpr/ppermute | solution.py:12
  197.9 3.1 %collective-permute-done = bf16[128,128]{1,0:T(8,128)(2,1)S(1)} collective-permute-done((bf16[128,128]{1,0:T(8,128)(2,1)S(1)}, bf16[128,128]{1,0:T(8,128)(2,1)S(1)}, u32[]{:S(2)}, u32[]{:S(2)}) %collective-permute-start) | collective-permute-done | bytes 32800 | tf_op jit(solution)/shard_map/while/body/eval_jaxpr/ppermute | solution.py:12
  201.4 2.4 %collective-permute-done.2 = f32[128,128]{1,0:T(8,128)S(1)} collective-permute-done((f32[128,128]{1,0:T(8,128)S(1)}, f32[128,128]{1,0:T(8,128)S(1)}, u32[]{:S(2)}, u32[]{:S(2)}) %collective-permute-start.2) | collective-permute-done | bytes 65568 | tf_op jit(solution)/shard_map/while/body/eval_jaxpr/ppermute | solution.py:12
  207.5 3.1 %collective-permute-done = bf16[128,128]{1,0:T(8,128)(2,1)S(1)} collective-permute-done((bf16[128,128]{1,0:T(8,128)(2,1)S(1)}, bf16[128,128]{1,0:T(8,128)(2,1)S(1)}, u32[]{:S(2)}, u32[]{:S(2)}) %collective-permute-start) | collective-permute-done | bytes 32800 | tf_op jit(solution)/shard_map/while/body/eval_jaxpr/ppermute | solution.py:12
  210.9 2.4 %collective-permute-done.2 = f32[128,128]{1,0:T(8,128)S(1)} collective-permute-done((f32[128,128]{1,0:T(8,128)S(1)}, f32[128,128]{1,0:T(8,128)S(1)}, u32[]{:S(2)}, u32[]{:S(2)}) %collective-permute-start.2) | collective-permute-done | bytes 65568 | tf_op jit(solution)/shard_map/while/body/eval_jaxpr/ppermute | solution.py:12
  216.7 4.2 %collective-permute-done.5 = f32[128,128]{1,0:T(8,128)S(1)} collective-permute-done((f32[128,128]{1,0:T(8,128)S(1)}, f32[128,128]{1,0:T(8,128)S(1)}, u32[]{:S(2)}, u32[]{:S(2)}) %collective-permute-start.5) | collective-permute-done | bytes 65568 | tf_op jit(solution)/shard_map/ppermute | solution.py:12
  (505 shorter events, 66.0 us)
Async XLA Ops:
  69.3 6.1 %collective-permute-start = (bf16[128,128]{1,0:T(8,128)(2,1)S(1)}, bf16[128,128]{1,0:T(8,128)(2,1)S(1)}, u32[]{:S(2)}, u32[]{:S(2)}) collective-permute-start(bf16[128,128]{1,0:T(8,128)(2,1)S(1)} %copy.67), channel_id=1, source_target_pairs={{0,1},{1,2},{2,3},{3,4},{4,5},{5,6},{6,7},{7,8},{8,9},{9,10},{10,1... | collective-permute-start | bytes 98312 | tf_op jit(solution)/shard_map/while/body/eval_jaxpr/ppermute | solution.py:12
  73.4 6.4 %collective-permute-start.2 = (f32[128,128]{1,0:T(8,128)S(1)}, f32[128,128]{1,0:T(8,128)S(1)}, u32[]{:S(2)}, u32[]{:S(2)}) collective-permute-start(f32[128,128]{1,0:T(8,128)S(1)} %fusion.122), channel_id=1, source_target_pairs={{0,1},{1,2},{2,3},{3,4},{4,5},{5,6},{6,7},{7,8},{8,9},{9,10},{10,1... | collective-permute-start | bytes 196616 | tf_op jit(solution)/shard_map/while/body/eval_jaxpr/ppermute | solution.py:12
  74.1 6.5 %collective-permute-start.3 = (f32[128,128]{1,0:T(8,128)S(1)}, f32[128,128]{1,0:T(8,128)S(1)}, u32[]{:S(2)}, u32[]{:S(2)}) collective-permute-start(f32[128,128]{1,0:T(8,128)S(1)} %convolution_add_fusion.6), channel_id=1, source_target_pairs={{0,1},{1,2},{2,3},{3,4},{4,5},{5,6},{6,7},{7,8},{8,9},{9,10},{10,1... | collective-permute-start | bytes 196616 | tf_op jit(solution)/shard_map/while/body/eval_jaxpr/ppermute | solution.py:12
  80.6 6.4 %collective-permute-start.1 = (bf16[128,128]{1,0:T(8,128)(2,1)S(1)}, bf16[128,128]{1,0:T(8,128)(2,1)S(1)}, u32[]{:S(2)}, u32[]{:S(2)}) collective-permute-start(bf16[128,128]{1,0:T(8,128)(2,1)S(1)} %copy.68), channel_id=1, source_target_pairs={{0,1},{1,2},{2,3},{3,4},{4,5},{5,6},{6,7},{7,8},{8,9},{9,10},{10,1... | collective-permute-start | bytes 98312 | tf_op jit(solution)/shard_map/while/body/eval_jaxpr/ppermute | solution.py:12
  83.0 6.4 %collective-permute-start.2 = (f32[128,128]{1,0:T(8,128)S(1)}, f32[128,128]{1,0:T(8,128)S(1)}, u32[]{:S(2)}, u32[]{:S(2)}) collective-permute-start(f32[128,128]{1,0:T(8,128)S(1)} %fusion.122), channel_id=1, source_target_pairs={{0,1},{1,2},{2,3},{3,4},{4,5},{5,6},{6,7},{7,8},{8,9},{9,10},{10,1... | collective-permute-start | bytes 196616 | tf_op jit(solution)/shard_map/while/body/eval_jaxpr/ppermute | solution.py:12
  83.3 6.8 %collective-permute-start.3 = (f32[128,128]{1,0:T(8,128)S(1)}, f32[128,128]{1,0:T(8,128)S(1)}, u32[]{:S(2)}, u32[]{:S(2)}) collective-permute-start(f32[128,128]{1,0:T(8,128)S(1)} %convolution_add_fusion.6), channel_id=1, source_target_pairs={{0,1},{1,2},{2,3},{3,4},{4,5},{5,6},{6,7},{7,8},{8,9},{9,10},{10,1... | collective-permute-start | bytes 196616 | tf_op jit(solution)/shard_map/while/body/eval_jaxpr/ppermute | solution.py:12
  90.1 6.4 %collective-permute-start.1 = (bf16[128,128]{1,0:T(8,128)(2,1)S(1)}, bf16[128,128]{1,0:T(8,128)(2,1)S(1)}, u32[]{:S(2)}, u32[]{:S(2)}) collective-permute-start(bf16[128,128]{1,0:T(8,128)(2,1)S(1)} %copy.68), channel_id=1, source_target_pairs={{0,1},{1,2},{2,3},{3,4},{4,5},{5,6},{6,7},{7,8},{8,9},{9,10},{10,1... | collective-permute-start | bytes 98312 | tf_op jit(solution)/shard_map/while/body/eval_jaxpr/ppermute | solution.py:12
  92.5 6.4 %collective-permute-start.2 = (f32[128,128]{1,0:T(8,128)S(1)}, f32[128,128]{1,0:T(8,128)S(1)}, u32[]{:S(2)}, u32[]{:S(2)}) collective-permute-start(f32[128,128]{1,0:T(8,128)S(1)} %fusion.122), channel_id=1, source_target_pairs={{0,1},{1,2},{2,3},{3,4},{4,5},{5,6},{6,7},{7,8},{8,9},{9,10},{10,1... | collective-permute-start | bytes 196616 | tf_op jit(solution)/shard_map/while/body/eval_jaxpr/ppermute | solution.py:12
  92.8 6.8 %collective-permute-start.3 = (f32[128,128]{1,0:T(8,128)S(1)}, f32[128,128]{1,0:T(8,128)S(1)}, u32[]{:S(2)}, u32[]{:S(2)}) collective-permute-start(f32[128,128]{1,0:T(8,128)S(1)} %convolution_add_fusion.6), channel_id=1, source_target_pairs={{0,1},{1,2},{2,3},{3,4},{4,5},{5,6},{6,7},{7,8},{8,9},{9,10},{10,1... | collective-permute-start | bytes 196616 | tf_op jit(solution)/shard_map/while/body/eval_jaxpr/ppermute | solution.py:12
  99.7 6.4 %collective-permute-start.1 = (bf16[128,128]{1,0:T(8,128)(2,1)S(1)}, bf16[128,128]{1,0:T(8,128)(2,1)S(1)}, u32[]{:S(2)}, u32[]{:S(2)}) collective-permute-start(bf16[128,128]{1,0:T(8,128)(2,1)S(1)} %copy.68), channel_id=1, source_target_pairs={{0,1},{1,2},{2,3},{3,4},{4,5},{5,6},{6,7},{7,8},{8,9},{9,10},{10,1... | collective-permute-start | bytes 98312 | tf_op jit(solution)/shard_map/while/body/eval_jaxpr/ppermute | solution.py:12
  102.0 6.4 %collective-permute-start.2 = (f32[128,128]{1,0:T(8,128)S(1)}, f32[128,128]{1,0:T(8,128)S(1)}, u32[]{:S(2)}, u32[]{:S(2)}) collective-permute-start(f32[128,128]{1,0:T(8,128)S(1)} %fusion.122), channel_id=1, source_target_pairs={{0,1},{1,2},{2,3},{3,4},{4,5},{5,6},{6,7},{7,8},{8,9},{9,10},{10,1... | collective-permute-start | bytes 196616 | tf_op jit(solution)/shard_map/while/body/eval_jaxpr/ppermute | solution.py:12
  102.3 6.8 %collective-permute-start.3 = (f32[128,128]{1,0:T(8,128)S(1)}, f32[128,128]{1,0:T(8,128)S(1)}, u32[]{:S(2)}, u32[]{:S(2)}) collective-permute-start(f32[128,128]{1,0:T(8,128)S(1)} %convolution_add_fusion.6), channel_id=1, source_target_pairs={{0,1},{1,2},{2,3},{3,4},{4,5},{5,6},{6,7},{7,8},{8,9},{9,10},{10,1... | collective-permute-start | bytes 196616 | tf_op jit(solution)/shard_map/while/body/eval_jaxpr/ppermute | solution.py:12
  109.2 6.4 %collective-permute-start.1 = (bf16[128,128]{1,0:T(8,128)(2,1)S(1)}, bf16[128,128]{1,0:T(8,128)(2,1)S(1)}, u32[]{:S(2)}, u32[]{:S(2)}) collective-permute-start(bf16[128,128]{1,0:T(8,128)(2,1)S(1)} %copy.68), channel_id=1, source_target_pairs={{0,1},{1,2},{2,3},{3,4},{4,5},{5,6},{6,7},{7,8},{8,9},{9,10},{10,1... | collective-permute-start | bytes 98312 | tf_op jit(solution)/shard_map/while/body/eval_jaxpr/ppermute | solution.py:12
  111.6 6.4 %collective-permute-start.2 = (f32[128,128]{1,0:T(8,128)S(1)}, f32[128,128]{1,0:T(8,128)S(1)}, u32[]{:S(2)}, u32[]{:S(2)}) collective-permute-start(f32[128,128]{1,0:T(8,128)S(1)} %fusion.122), channel_id=1, source_target_pairs={{0,1},{1,2},{2,3},{3,4},{4,5},{5,6},{6,7},{7,8},{8,9},{9,10},{10,1... | collective-permute-start | bytes 196616 | tf_op jit(solution)/shard_map/while/body/eval_jaxpr/ppermute | solution.py:12
  111.9 6.8 %collective-permute-start.3 = (f32[128,128]{1,0:T(8,128)S(1)}, f32[128,128]{1,0:T(8,128)S(1)}, u32[]{:S(2)}, u32[]{:S(2)}) collective-permute-start(f32[128,128]{1,0:T(8,128)S(1)} %convolution_add_fusion.6), channel_id=1, source_target_pairs={{0,1},{1,2},{2,3},{3,4},{4,5},{5,6},{6,7},{7,8},{8,9},{9,10},{10,1... | collective-permute-start | bytes 196616 | tf_op jit(solution)/shard_map/while/body/eval_jaxpr/ppermute | solution.py:12
  118.7 6.4 %collective-permute-start.1 = (bf16[128,128]{1,0:T(8,128)(2,1)S(1)}, bf16[128,128]{1,0:T(8,128)(2,1)S(1)}, u32[]{:S(2)}, u32[]{:S(2)}) collective-permute-start(bf16[128,128]{1,0:T(8,128)(2,1)S(1)} %copy.68), channel_id=1, source_target_pairs={{0,1},{1,2},{2,3},{3,4},{4,5},{5,6},{6,7},{7,8},{8,9},{9,10},{10,1... | collective-permute-start | bytes 98312 | tf_op jit(solution)/shard_map/while/body/eval_jaxpr/ppermute | solution.py:12
  121.1 6.4 %collective-permute-start.2 = (f32[128,128]{1,0:T(8,128)S(1)}, f32[128,128]{1,0:T(8,128)S(1)}, u32[]{:S(2)}, u32[]{:S(2)}) collective-permute-start(f32[128,128]{1,0:T(8,128)S(1)} %fusion.122), channel_id=1, source_target_pairs={{0,1},{1,2},{2,3},{3,4},{4,5},{5,6},{6,7},{7,8},{8,9},{9,10},{10,1... | collective-permute-start | bytes 196616 | tf_op jit(solution)/shard_map/while/body/eval_jaxpr/ppermute | solution.py:12
  121.4 6.8 %collective-permute-start.3 = (f32[128,128]{1,0:T(8,128)S(1)}, f32[128,128]{1,0:T(8,128)S(1)}, u32[]{:S(2)}, u32[]{:S(2)}) collective-permute-start(f32[128,128]{1,0:T(8,128)S(1)} %convolution_add_fusion.6), channel_id=1, source_target_pairs={{0,1},{1,2},{2,3},{3,4},{4,5},{5,6},{6,7},{7,8},{8,9},{9,10},{10,1... | collective-permute-start | bytes 196616 | tf_op jit(solution)/shard_map/while/body/eval_jaxpr/ppermute | solution.py:12
  128.3 6.4 %collective-permute-start.1 = (bf16[128,128]{1,0:T(8,128)(2,1)S(1)}, bf16[128,128]{1,0:T(8,128)(2,1)S(1)}, u32[]{:S(2)}, u32[]{:S(2)}) collective-permute-start(bf16[128,128]{1,0:T(8,128)(2,1)S(1)} %copy.68), channel_id=1, source_target_pairs={{0,1},{1,2},{2,3},{3,4},{4,5},{5,6},{6,7},{7,8},{8,9},{9,10},{10,1... | collective-permute-start | bytes 98312 | tf_op jit(solution)/shard_map/while/body/eval_jaxpr/ppermute | solution.py:12
  130.6 6.4 %collective-permute-start.2 = (f32[128,128]{1,0:T(8,128)S(1)}, f32[128,128]{1,0:T(8,128)S(1)}, u32[]{:S(2)}, u32[]{:S(2)}) collective-permute-start(f32[128,128]{1,0:T(8,128)S(1)} %fusion.122), channel_id=1, source_target_pairs={{0,1},{1,2},{2,3},{3,4},{4,5},{5,6},{6,7},{7,8},{8,9},{9,10},{10,1... | collective-permute-start | bytes 196616 | tf_op jit(solution)/shard_map/while/body/eval_jaxpr/ppermute | solution.py:12
  130.9 6.8 %collective-permute-start.3 = (f32[128,128]{1,0:T(8,128)S(1)}, f32[128,128]{1,0:T(8,128)S(1)}, u32[]{:S(2)}, u32[]{:S(2)}) collective-permute-start(f32[128,128]{1,0:T(8,128)S(1)} %convolution_add_fusion.6), channel_id=1, source_target_pairs={{0,1},{1,2},{2,3},{3,4},{4,5},{5,6},{6,7},{7,8},{8,9},{9,10},{10,1... | collective-permute-start | bytes 196616 | tf_op jit(solution)/shard_map/while/body/eval_jaxpr/ppermute | solution.py:12
  137.8 6.4 %collective-permute-start.1 = (bf16[128,128]{1,0:T(8,128)(2,1)S(1)}, bf16[128,128]{1,0:T(8,128)(2,1)S(1)}, u32[]{:S(2)}, u32[]{:S(2)}) collective-permute-start(bf16[128,128]{1,0:T(8,128)(2,1)S(1)} %copy.68), channel_id=1, source_target_pairs={{0,1},{1,2},{2,3},{3,4},{4,5},{5,6},{6,7},{7,8},{8,9},{9,10},{10,1... | collective-permute-start | bytes 98312 | tf_op jit(solution)/shard_map/while/body/eval_jaxpr/ppermute | solution.py:12
  140.2 6.4 %collective-permute-start.2 = (f32[128,128]{1,0:T(8,128)S(1)}, f32[128,128]{1,0:T(8,128)S(1)}, u32[]{:S(2)}, u32[]{:S(2)}) collective-permute-start(f32[128,128]{1,0:T(8,128)S(1)} %fusion.122), channel_id=1, source_target_pairs={{0,1},{1,2},{2,3},{3,4},{4,5},{5,6},{6,7},{7,8},{8,9},{9,10},{10,1... | collective-permute-start | bytes 196616 | tf_op jit(solution)/shard_map/while/body/eval_jaxpr/ppermute | solution.py:12
  140.5 6.8 %collective-permute-start.3 = (f32[128,128]{1,0:T(8,128)S(1)}, f32[128,128]{1,0:T(8,128)S(1)}, u32[]{:S(2)}, u32[]{:S(2)}) collective-permute-start(f32[128,128]{1,0:T(8,128)S(1)} %convolution_add_fusion.6), channel_id=1, source_target_pairs={{0,1},{1,2},{2,3},{3,4},{4,5},{5,6},{6,7},{7,8},{8,9},{9,10},{10,1... | collective-permute-start | bytes 196616 | tf_op jit(solution)/shard_map/while/body/eval_jaxpr/ppermute | solution.py:12
  147.3 6.4 %collective-permute-start.1 = (bf16[128,128]{1,0:T(8,128)(2,1)S(1)}, bf16[128,128]{1,0:T(8,128)(2,1)S(1)}, u32[]{:S(2)}, u32[]{:S(2)}) collective-permute-start(bf16[128,128]{1,0:T(8,128)(2,1)S(1)} %copy.68), channel_id=1, source_target_pairs={{0,1},{1,2},{2,3},{3,4},{4,5},{5,6},{6,7},{7,8},{8,9},{9,10},{10,1... | collective-permute-start | bytes 98312 | tf_op jit(solution)/shard_map/while/body/eval_jaxpr/ppermute | solution.py:12
  149.7 6.4 %collective-permute-start.2 = (f32[128,128]{1,0:T(8,128)S(1)}, f32[128,128]{1,0:T(8,128)S(1)}, u32[]{:S(2)}, u32[]{:S(2)}) collective-permute-start(f32[128,128]{1,0:T(8,128)S(1)} %fusion.122), channel_id=1, source_target_pairs={{0,1},{1,2},{2,3},{3,4},{4,5},{5,6},{6,7},{7,8},{8,9},{9,10},{10,1... | collective-permute-start | bytes 196616 | tf_op jit(solution)/shard_map/while/body/eval_jaxpr/ppermute | solution.py:12
  150.0 6.8 %collective-permute-start.3 = (f32[128,128]{1,0:T(8,128)S(1)}, f32[128,128]{1,0:T(8,128)S(1)}, u32[]{:S(2)}, u32[]{:S(2)}) collective-permute-start(f32[128,128]{1,0:T(8,128)S(1)} %convolution_add_fusion.6), channel_id=1, source_target_pairs={{0,1},{1,2},{2,3},{3,4},{4,5},{5,6},{6,7},{7,8},{8,9},{9,10},{10,1... | collective-permute-start | bytes 196616 | tf_op jit(solution)/shard_map/while/body/eval_jaxpr/ppermute | solution.py:12
  156.9 6.4 %collective-permute-start.1 = (bf16[128,128]{1,0:T(8,128)(2,1)S(1)}, bf16[128,128]{1,0:T(8,128)(2,1)S(1)}, u32[]{:S(2)}, u32[]{:S(2)}) collective-permute-start(bf16[128,128]{1,0:T(8,128)(2,1)S(1)} %copy.68), channel_id=1, source_target_pairs={{0,1},{1,2},{2,3},{3,4},{4,5},{5,6},{6,7},{7,8},{8,9},{9,10},{10,1... | collective-permute-start | bytes 98312 | tf_op jit(solution)/shard_map/while/body/eval_jaxpr/ppermute | solution.py:12
  159.2 6.4 %collective-permute-start.2 = (f32[128,128]{1,0:T(8,128)S(1)}, f32[128,128]{1,0:T(8,128)S(1)}, u32[]{:S(2)}, u32[]{:S(2)}) collective-permute-start(f32[128,128]{1,0:T(8,128)S(1)} %fusion.122), channel_id=1, source_target_pairs={{0,1},{1,2},{2,3},{3,4},{4,5},{5,6},{6,7},{7,8},{8,9},{9,10},{10,1... | collective-permute-start | bytes 196616 | tf_op jit(solution)/shard_map/while/body/eval_jaxpr/ppermute | solution.py:12
  159.5 6.8 %collective-permute-start.3 = (f32[128,128]{1,0:T(8,128)S(1)}, f32[128,128]{1,0:T(8,128)S(1)}, u32[]{:S(2)}, u32[]{:S(2)}) collective-permute-start(f32[128,128]{1,0:T(8,128)S(1)} %convolution_add_fusion.6), channel_id=1, source_target_pairs={{0,1},{1,2},{2,3},{3,4},{4,5},{5,6},{6,7},{7,8},{8,9},{9,10},{10,1... | collective-permute-start | bytes 196616 | tf_op jit(solution)/shard_map/while/body/eval_jaxpr/ppermute | solution.py:12
  166.4 6.4 %collective-permute-start.1 = (bf16[128,128]{1,0:T(8,128)(2,1)S(1)}, bf16[128,128]{1,0:T(8,128)(2,1)S(1)}, u32[]{:S(2)}, u32[]{:S(2)}) collective-permute-start(bf16[128,128]{1,0:T(8,128)(2,1)S(1)} %copy.68), channel_id=1, source_target_pairs={{0,1},{1,2},{2,3},{3,4},{4,5},{5,6},{6,7},{7,8},{8,9},{9,10},{10,1... | collective-permute-start | bytes 98312 | tf_op jit(solution)/shard_map/while/body/eval_jaxpr/ppermute | solution.py:12
  168.8 6.4 %collective-permute-start.2 = (f32[128,128]{1,0:T(8,128)S(1)}, f32[128,128]{1,0:T(8,128)S(1)}, u32[]{:S(2)}, u32[]{:S(2)}) collective-permute-start(f32[128,128]{1,0:T(8,128)S(1)} %fusion.122), channel_id=1, source_target_pairs={{0,1},{1,2},{2,3},{3,4},{4,5},{5,6},{6,7},{7,8},{8,9},{9,10},{10,1... | collective-permute-start | bytes 196616 | tf_op jit(solution)/shard_map/while/body/eval_jaxpr/ppermute | solution.py:12
  169.1 6.8 %collective-permute-start.3 = (f32[128,128]{1,0:T(8,128)S(1)}, f32[128,128]{1,0:T(8,128)S(1)}, u32[]{:S(2)}, u32[]{:S(2)}) collective-permute-start(f32[128,128]{1,0:T(8,128)S(1)} %convolution_add_fusion.6), channel_id=1, source_target_pairs={{0,1},{1,2},{2,3},{3,4},{4,5},{5,6},{6,7},{7,8},{8,9},{9,10},{10,1... | collective-permute-start | bytes 196616 | tf_op jit(solution)/shard_map/while/body/eval_jaxpr/ppermute | solution.py:12
  175.9 6.0 %collective-permute-start = (bf16[128,128]{1,0:T(8,128)(2,1)S(1)}, bf16[128,128]{1,0:T(8,128)(2,1)S(1)}, u32[]{:S(2)}, u32[]{:S(2)}) collective-permute-start(bf16[128,128]{1,0:T(8,128)(2,1)S(1)} %copy.67), channel_id=1, source_target_pairs={{0,1},{1,2},{2,3},{3,4},{4,5},{5,6},{6,7},{7,8},{8,9},{9,10},{10,1... | collective-permute-start | bytes 98312 | tf_op jit(solution)/shard_map/while/body/eval_jaxpr/ppermute | solution.py:12
  175.9 6.4 %collective-permute-start.1 = (bf16[128,128]{1,0:T(8,128)(2,1)S(1)}, bf16[128,128]{1,0:T(8,128)(2,1)S(1)}, u32[]{:S(2)}, u32[]{:S(2)}) collective-permute-start(bf16[128,128]{1,0:T(8,128)(2,1)S(1)} %copy.68), channel_id=1, source_target_pairs={{0,1},{1,2},{2,3},{3,4},{4,5},{5,6},{6,7},{7,8},{8,9},{9,10},{10,1... | collective-permute-start | bytes 98312 | tf_op jit(solution)/shard_map/while/body/eval_jaxpr/ppermute | solution.py:12
  178.3 6.4 %collective-permute-start.2 = (f32[128,128]{1,0:T(8,128)S(1)}, f32[128,128]{1,0:T(8,128)S(1)}, u32[]{:S(2)}, u32[]{:S(2)}) collective-permute-start(f32[128,128]{1,0:T(8,128)S(1)} %fusion.122), channel_id=1, source_target_pairs={{0,1},{1,2},{2,3},{3,4},{4,5},{5,6},{6,7},{7,8},{8,9},{9,10},{10,1... | collective-permute-start | bytes 196616 | tf_op jit(solution)/shard_map/while/body/eval_jaxpr/ppermute | solution.py:12
  178.6 6.8 %collective-permute-start.3 = (f32[128,128]{1,0:T(8,128)S(1)}, f32[128,128]{1,0:T(8,128)S(1)}, u32[]{:S(2)}, u32[]{:S(2)}) collective-permute-start(f32[128,128]{1,0:T(8,128)S(1)} %convolution_add_fusion.6), channel_id=1, source_target_pairs={{0,1},{1,2},{2,3},{3,4},{4,5},{5,6},{6,7},{7,8},{8,9},{9,10},{10,1... | collective-permute-start | bytes 196616 | tf_op jit(solution)/shard_map/while/body/eval_jaxpr/ppermute | solution.py:12
  185.5 6.4 %collective-permute-start.1 = (bf16[128,128]{1,0:T(8,128)(2,1)S(1)}, bf16[128,128]{1,0:T(8,128)(2,1)S(1)}, u32[]{:S(2)}, u32[]{:S(2)}) collective-permute-start(bf16[128,128]{1,0:T(8,128)(2,1)S(1)} %copy.68), channel_id=1, source_target_pairs={{0,1},{1,2},{2,3},{3,4},{4,5},{5,6},{6,7},{7,8},{8,9},{9,10},{10,1... | collective-permute-start | bytes 98312 | tf_op jit(solution)/shard_map/while/body/eval_jaxpr/ppermute | solution.py:12
  187.8 6.4 %collective-permute-start.2 = (f32[128,128]{1,0:T(8,128)S(1)}, f32[128,128]{1,0:T(8,128)S(1)}, u32[]{:S(2)}, u32[]{:S(2)}) collective-permute-start(f32[128,128]{1,0:T(8,128)S(1)} %fusion.122), channel_id=1, source_target_pairs={{0,1},{1,2},{2,3},{3,4},{4,5},{5,6},{6,7},{7,8},{8,9},{9,10},{10,1... | collective-permute-start | bytes 196616 | tf_op jit(solution)/shard_map/while/body/eval_jaxpr/ppermute | solution.py:12
  188.1 6.8 %collective-permute-start.3 = (f32[128,128]{1,0:T(8,128)S(1)}, f32[128,128]{1,0:T(8,128)S(1)}, u32[]{:S(2)}, u32[]{:S(2)}) collective-permute-start(f32[128,128]{1,0:T(8,128)S(1)} %convolution_add_fusion.6), channel_id=1, source_target_pairs={{0,1},{1,2},{2,3},{3,4},{4,5},{5,6},{6,7},{7,8},{8,9},{9,10},{10,1... | collective-permute-start | bytes 196616 | tf_op jit(solution)/shard_map/while/body/eval_jaxpr/ppermute | solution.py:12
  195.0 6.4 %collective-permute-start.1 = (bf16[128,128]{1,0:T(8,128)(2,1)S(1)}, bf16[128,128]{1,0:T(8,128)(2,1)S(1)}, u32[]{:S(2)}, u32[]{:S(2)}) collective-permute-start(bf16[128,128]{1,0:T(8,128)(2,1)S(1)} %copy.68), channel_id=1, source_target_pairs={{0,1},{1,2},{2,3},{3,4},{4,5},{5,6},{6,7},{7,8},{8,9},{9,10},{10,1... | collective-permute-start | bytes 98312 | tf_op jit(solution)/shard_map/while/body/eval_jaxpr/ppermute | solution.py:12
  197.4 6.4 %collective-permute-start.2 = (f32[128,128]{1,0:T(8,128)S(1)}, f32[128,128]{1,0:T(8,128)S(1)}, u32[]{:S(2)}, u32[]{:S(2)}) collective-permute-start(f32[128,128]{1,0:T(8,128)S(1)} %fusion.122), channel_id=1, source_target_pairs={{0,1},{1,2},{2,3},{3,4},{4,5},{5,6},{6,7},{7,8},{8,9},{9,10},{10,1... | collective-permute-start | bytes 196616 | tf_op jit(solution)/shard_map/while/body/eval_jaxpr/ppermute | solution.py:12
  197.7 6.8 %collective-permute-start.3 = (f32[128,128]{1,0:T(8,128)S(1)}, f32[128,128]{1,0:T(8,128)S(1)}, u32[]{:S(2)}, u32[]{:S(2)}) collective-permute-start(f32[128,128]{1,0:T(8,128)S(1)} %convolution_add_fusion.6), channel_id=1, source_target_pairs={{0,1},{1,2},{2,3},{3,4},{4,5},{5,6},{6,7},{7,8},{8,9},{9,10},{10,1... | collective-permute-start | bytes 196616 | tf_op jit(solution)/shard_map/while/body/eval_jaxpr/ppermute | solution.py:12
  204.5 6.4 %collective-permute-start.1 = (bf16[128,128]{1,0:T(8,128)(2,1)S(1)}, bf16[128,128]{1,0:T(8,128)(2,1)S(1)}, u32[]{:S(2)}, u32[]{:S(2)}) collective-permute-start(bf16[128,128]{1,0:T(8,128)(2,1)S(1)} %copy.68), channel_id=1, source_target_pairs={{0,1},{1,2},{2,3},{3,4},{4,5},{5,6},{6,7},{7,8},{8,9},{9,10},{10,1... | collective-permute-start | bytes 98312 | tf_op jit(solution)/shard_map/while/body/eval_jaxpr/ppermute | solution.py:12
  206.9 6.4 %collective-permute-start.2 = (f32[128,128]{1,0:T(8,128)S(1)}, f32[128,128]{1,0:T(8,128)S(1)}, u32[]{:S(2)}, u32[]{:S(2)}) collective-permute-start(f32[128,128]{1,0:T(8,128)S(1)} %fusion.122), channel_id=1, source_target_pairs={{0,1},{1,2},{2,3},{3,4},{4,5},{5,6},{6,7},{7,8},{8,9},{9,10},{10,1... | collective-permute-start | bytes 196616 | tf_op jit(solution)/shard_map/while/body/eval_jaxpr/ppermute | solution.py:12
  207.2 6.8 %collective-permute-start.3 = (f32[128,128]{1,0:T(8,128)S(1)}, f32[128,128]{1,0:T(8,128)S(1)}, u32[]{:S(2)}, u32[]{:S(2)}) collective-permute-start(f32[128,128]{1,0:T(8,128)S(1)} %convolution_add_fusion.6), channel_id=1, source_target_pairs={{0,1},{1,2},{2,3},{3,4},{4,5},{5,6},{6,7},{7,8},{8,9},{9,10},{10,1... | collective-permute-start | bytes 196616 | tf_op jit(solution)/shard_map/while/body/eval_jaxpr/ppermute | solution.py:12
  214.5 6.4 %collective-permute-start.5 = (f32[128,128]{1,0:T(8,128)S(1)}, f32[128,128]{1,0:T(8,128)S(1)}, u32[]{:S(2)}, u32[]{:S(2)}) collective-permute-start(f32[128,128]{1,0:T(8,128)S(1)} %convolution_add_fusion.2), channel_id=1, source_target_pairs={{0,1},{1,2},{2,3},{3,4},{4,5},{5,6},{6,7},{7,8},{8,9},{9,10},{10,1... | collective-permute-start | bytes 196616 | tf_op jit(solution)/shard_map/ppermute | solution.py:12
  215.0 6.7 %collective-permute-start.4 = (f32[128,128]{1,0:T(8,128)S(1)}, f32[128,128]{1,0:T(8,128)S(1)}, u32[]{:S(2)}, u32[]{:S(2)}) collective-permute-start(f32[128,128]{1,0:T(8,128)S(1)} %fusion.45), channel_id=1, source_target_pairs={{0,1},{1,2},{2,3},{3,4},{4,5},{5,6},{6,7},{7,8},{8,9},{9,10},{10,1... | collective-permute-start | bytes 196616 | tf_op jit(solution)/shard_map/ppermute | solution.py:12
  (18 other events, 109.8 us)
where the time goes:
time: 223 us
  waiting for transfers between devices  103 us (46%)
  blocking collectives  43.4 us (19%)
  matrix products  31.7 us (14%)
  local copies, waits for them, and re-layouts  17 us (8%)
  loops' own time  13 us (6%)
  other arithmetic  5.81 us (3%)
  starting transfers between devices  5 us (2%)
  between operations  4.08 us (2%)
    ppermute x62, waiting for transfers between devices, passed_along(): return lax.ppermute(value, axis, pairs)  103 us
    all_gather x1, blocking collectives, shards(): key_piece = lax.all_gather(key_states, 'blk', axis=0, tiled=True)  24.6 us
    all_gather x1, blocking collectives, shards(): value_piece = lax.all_gather(value_states, 'blk', axis=0, tiled=True)  18.9 us
    another operation x1, loops' own time, shards(): carry_state = lax.fori_loop(0, cycle_size - 1, key_turn, carry_state)  11.7 us
    dynamic_slice x16, local copies, waits for them, and re-layouts, key_step(): key_pos = block_order[source] * tok_rows + offsets  9.38 us
    dot_general x32, matrix products, mask_for(): jnp.dot(tile_rows, one_hot.T, preferred_element_type=jnp.float32) > 0.5  6.53 us
    ppermute x62, starting transfers between devices, passed_along(): return lax.ppermute(value, axis, pairs)  5 us
    dot_general x16, matrix products, softmax_update(): jnp.dot(weights.astype(jnp.bfloat16), value_sub, preferred_element_type=j...  4.83 us
  transfers between devices with their start and end apart: 62, of which 62 were waited for; matrix products, arithmetic and copies ran while one was open for 14% of the time, Pallas kernels for 0%

commit v1 on v0

--- a/solution.py
+++ b/solution.py
@@ -81,7 +81,32 @@
         jnp.zeros((total_rows, head_width), jnp.float32),
     )
     key_piece = lax.all_gather(key_states, "blk", axis=0, tiled=True)
-    value_piece = lax.all_gather(value_states, "blk", axis=0, tiled=True)
+
+    def number_the_tasks(buf):
+        axis_name = "blk"
+        local_out = jax.lax.psum(1, axis_name)
+        h_now, y2, val2 = (local_out, jax.lax.axis_index(axis_name), buf.shape[0])
+        copies = [src_i * h_now if s == 0 else src_i for s, src_i in enumerate(buf.shape)]
+        part_next = jnp.zeros(copies, buf.dtype)
+        clean = lax.dynamic_update_slice_in_dim(part_next, buf, y2 * val2, axis=0)
+        local_next = all_rows = buf
+        for c in range(1, h_now // 2 + 1):
+            local_next = jax.lax.ppermute(
+                local_next, axis_name, [(s, (s + 1) % h_now) for s in range(h_now)]
+            )
+            clean = lax.dynamic_update_slice_in_dim(
+                clean, local_next, (y2 - c) % h_now * val2, axis=0
+            )
+            if 2 * c < h_now:
+                all_rows = jax.lax.ppermute(
+                    all_rows, axis_name, [(s, (s - 1) % h_now) for s in range(h_now)]
+                )
+                clean = lax.dynamic_update_slice_in_dim(
+                    clean, all_rows, (y2 + c) % h_now * val2, axis=0
+                )
+        return clean
+
+    value_piece = number_the_tasks(value_states)
     piece_rows = key_piece.shape[0]
 
     def sub_step(sub_num, inner_state):

time: 223 us -> 247 us (1.11)
  starting transfers between devices: 5 us -> 35 us
  blocking collectives: 43.4 us -> 20.9 us
  waiting for transfers between devices: 103 us -> 119 us
    ppermute x0 -> x15, starting transfers between devices: none -> 32.2 us  [the longest x7 31.3 us: number_the_tasks(): jax.lax.ppermute(all_rows, axis_name, [(s, (s - 1) % h_now) for s in rang...]
    all_gather x1 -> x0, blocking collectives: 18.9 us -> none  [shards(): value_piece = lax.all_gather(value_states, 'blk', axis=0, tiled=True)]
    ppermute x0 -> x15, waiting for transfers between devices: none -> 15.4 us  [the longest x8 15.4 us: number_the_tasks(): jax.lax.ppermute(local_next, axis_name, [(s, (s + 1) % h_now) for s in ra...]
    all_gather x1, blocking collectives: 24.6 us -> 20.9 us  [shards(): key_piece = lax.all_gather(key_states, 'blk', axis=0, tiled=True)]
  transfers between devices with their start and end apart: 62 -> 77, of which waited for: 62 -> 69; matrix products, arithmetic and copies ran while one was open for 14% -> 14% of each run, Pallas kernels for 0% -> 0%
where the time goes in v1:
time: 247 us
  waiting for transfers between devices  119 us (48%)
  starting transfers between devices  35 us (14%)
  matrix products  31.7 us (13%)
  blocking collectives  20.9 us (8%)
  local copies, waits for them, and re-layouts  17.3 us (7%)
  loops' own time  13.1 us (5%)
  other arithmetic  5.81 us (2%)
  between operations  4.18 us (2%)
    ppermute x62, waiting for transfers between devices, passed_along(): return lax.ppermute(value, axis, pairs)  103 us
    ppermute x7, starting transfers between devices, number_the_tasks(): jax.lax.ppermute(all_rows, axis_name, [(s, (s - 1) % h_now) for s in rang...  31.3 us
    all_gather x1, blocking collectives, shards(): key_piece = lax.all_gather(key_states, 'blk', axis=0, tiled=True)  20.9 us
    ppermute x8, waiting for transfers between devices, number_the_tasks(): jax.lax.ppermute(local_next, axis_name, [(s, (s + 1) % h_now) for s in ra...  15.4 us
    another operation x1, loops' own time, shards(): carry_state = lax.fori_loop(0, cycle_size - 1, key_turn, carry_state)  11.8 us
    dynamic_slice x16, local copies, waits for them, and re-layouts, key_step(): key_pos = block_order[source] * tok_rows + offsets  9.39 us
    dot_general x32, matrix products, mask_for(): jnp.dot(tile_rows, one_hot.T, preferred_element_type=jnp.float32) > 0.5  6.53 us
  transfers between devices with their start and end apart: 77, of which 69 were waited for; matrix products, arithmetic and copies ran while one was open for 14% of the time, Pallas kernels for 0%

profile of v1, /device:TPU:0, one launch (start us, length us, event | category | flops | bytes accessed | tf_op | source)
XLA Modules:
  0.0 246.6 jit_solution(14956635678238291318)
XLA Ops:
  1.9 5.1 %collective-permute-start.5 = (bf16[128,128]{1,0:T(8,128)(2,1)S(1)}, bf16[128,128]{1,0:T(8,128)(2,1)S(1)}, u32[]{:S(2)}, u32[]{:S(2)}) collective-permute-start(bf16[128,128]{1,0:T(8,128)(2,1)S(1)} %copy.100), channel_id=1, source_target_pairs={{0,15},{1,0},{2,1},{3,2},{4,3},{5,4},{6,5},{7,6},{8,7},{9,8},{10,9... | collective-permute-start | bytes 98312 | tf_op jit(solution)/shard_map/ppermute | solution.py:101
  10.9 20.9 %all_gather.3 = bf16[2048,128]{1,0:T(8,128)(2,1)S(1)} all-gather(bf16[128,128]{1,0:T(8,128)(2,1)S(1)} %copy.99), channel_id=1, replica_groups=mesh['groups'=2,'blk'=16] {'blk'}, dimensions={0}, use_global_device_ids=true | all-gather | bytes 557056 | tf_op jit(solution)/shard_map/all_gather | solution.py:83
  34.8 4.1 %collective-permute-start.7 = (bf16[128,128]{1,0:T(8,128)(2,1)S(1)}, bf16[128,128]{1,0:T(8,128)(2,1)S(1)}, u32[]{:S(2)}, u32[]{:S(2)}) collective-permute-start(bf16[128,128]{1,0:T(8,128)(2,1)S(1)} %collective-permute-done.5), channel_id=1, source_target_pairs={{0,15},{1,0},{2,1},{3,2},{4,3},{5,4},{6,5},{7,6},{8,7},{9,8},{10,9... | collective-permute-start | bytes 98312 | tf_op jit(solution)/shard_map/ppermute | solution.py:101
  39.0 1.6 collective-permute-done.6
  40.5 4.4 %collective-permute-start.9 = (bf16[128,128]{1,0:T(8,128)(2,1)S(1)}, bf16[128,128]{1,0:T(8,128)(2,1)S(1)}, u32[]{:S(2)}, u32[]{:S(2)}) collective-permute-start(bf16[128,128]{1,0:T(8,128)(2,1)S(1)} %collective-permute-done.7), channel_id=1, source_target_pairs={{0,15},{1,0},{2,1},{3,2},{4,3},{5,4},{6,5},{7,6},{8,7},{9,8},{10,9... | collective-permute-start | bytes 98312 | tf_op jit(solution)/shard_map/ppermute | solution.py:101
  45.0 1.6 collective-permute-done.8
  46.6 4.4 %collective-permute-start.11 = (bf16[128,128]{1,0:T(8,128)(2,1)S(1)}, bf16[128,128]{1,0:T(8,128)(2,1)S(1)}, u32[]{:S(2)}, u32[]{:S(2)}) collective-permute-start(bf16[128,128]{1,0:T(8,128)(2,1)S(1)} %collective-permute-done.9), channel_id=1, source_target_pairs={{0,15},{1,0},{2,1},{3,2},{4,3},{5,4},{6,5},{7,6},{8,7},{9,8},{10,9... | collective-permute-start | bytes 98312 | tf_op jit(solution)/shard_map/ppermute | solution.py:101
  51.0 1.6 collective-permute-done.10
  52.6 4.4 %collective-permute-start.13 = (bf16[128,128]{1,0:T(8,128)(2,1)S(1)}, bf16[128,128]{1,0:T(8,128)(2,1)S(1)}, u32[]{:S(2)}, u32[]{:S(2)}) collective-permute-start(bf16[128,128]{1,0:T(8,128)(2,1)S(1)} %collective-permute-done.11), channel_id=1, source_target_pairs={{0,15},{1,0},{2,1},{3,2},{4,3},{5,4},{6,5},{7,6},{8,7},{9,8},{10,9... | collective-permute-start | bytes 98312 | tf_op jit(solution)/shard_map/ppermute | solution.py:101
  57.1 1.6 collective-permute-done.12
  58.6 4.4 %collective-permute-start.15 = (bf16[128,128]{1,0:T(8,128)(2,1)S(1)}, bf16[128,128]{1,0:T(8,128)(2,1)S(1)}, u32[]{:S(2)}, u32[]{:S(2)}) collective-permute-start(bf16[128,128]{1,0:T(8,128)(2,1)S(1)} %collective-permute-done.13), channel_id=1, source_target_pairs={{0,15},{1,0},{2,1},{3,2},{4,3},{5,4},{6,5},{7,6},{8,7},{9,8},{10,9... | collective-permute-start | bytes 98312 | tf_op jit(solution)/shard_map/ppermute | solution.py:101
  63.1 1.6 collective-permute-done.14
  64.7 4.4 %collective-permute-start.17 = (bf16[128,128]{1,0:T(8,128)(2,1)S(1)}, bf16[128,128]{1,0:T(8,128)(2,1)S(1)}, u32[]{:S(2)}, u32[]{:S(2)}) collective-permute-start(bf16[128,128]{1,0:T(8,128)(2,1)S(1)} %collective-permute-done.15), channel_id=1, source_target_pairs={{0,15},{1,0},{2,1},{3,2},{4,3},{5,4},{6,5},{7,6},{8,7},{9,8},{10,9... | collective-permute-start | bytes 98312 | tf_op jit(solution)/shard_map/ppermute | solution.py:101
  69.1 1.6 collective-permute-done.16
  70.8 6.0 %collective-permute-done.18 = bf16[128,128]{1,0:T(8,128)(2,1)S(1)} collective-permute-done((bf16[128,128]{1,0:T(8,128)(2,1)S(1)}, bf16[128,128]{1,0:T(8,128)(2,1)S(1)}, u32[]{:S(2)}, u32[]{:S(2)}) %collective-permute-start.18) | collective-permute-done | bytes 32800 | tf_op jit(solution)/shard_map/ppermute | solution.py:94
  76.8 17.6 %while.47 = (s32[]{:T(128)}, f32[512]{0:T(512)S(1)}, f32[512]{0:T(512)S(1)}, f32[512,128]{1,0:T(8,128)S(1)}, s32[]{:T(128)}, /*index=5*/s32[16]{0:T(128)S(1)}, b...) while((s32[]{:T(128)}, f32[512]{0:T(512)S(1)}, ...), condition=%wide.region_4.5_spmd.clone, body=%wide.region_0.4_spmd.clone.sunk | while | flops 34965508 | bytes 1841459 | solution.py:129
  94.7 143.1 %while.48 = (s32[]{:T(128)}, bf16[128,128]{1,0:T(8,128)(2,1)S(1)}, bf16[128,128]{1,0:T(8,128)(2,1)S(1)}, f32[128,128]{1,0:T(8,128)S(1)}, f32[128,128]{1,0:T(8,12...) while((s32[]{:T(128)}, bf16[128,128]{1,0:T(8,128)(2,1)S(1)}, ...), condition=%wide.region_7.8_spmd.clone.clone, body=%wide.region_6.7_spmd.clone.clone.sunk | while | flops 85202960 | bytes 3711538 | solution.py:180
  97.7 3.0 %collective-permute-done = bf16[128,128]{1,0:T(8,128)(2,1)S(1)} collective-permute-done((bf16[128,128]{1,0:T(8,128)(2,1)S(1)}, bf16[128,128]{1,0:T(8,128)(2,1)S(1)}, u32[]{:S(2)}, u32[]{:S(2)}) %collective-permute-start) | collective-permute-done | bytes 32800 | tf_op jit(solution)/shard_map/while/body/eval_jaxpr/ppermute | solution.py:12
  101.1 2.5 collective-permute-done.2
  107.3 3.1 %collective-permute-done = bf16[128,128]{1,0:T(8,128)(2,1)S(1)} collective-permute-done((bf16[128,128]{1,0:T(8,128)(2,1)S(1)}, bf16[128,128]{1,0:T(8,128)(2,1)S(1)}, u32[]{:S(2)}, u32[]{:S(2)}) %collective-permute-start) | collective-permute-done | bytes 32800 | tf_op jit(solution)/shard_map/while/body/eval_jaxpr/ppermute | solution.py:12
  110.7 2.4 collective-permute-done.2
  116.8 3.1 %collective-permute-done = bf16[128,128]{1,0:T(8,128)(2,1)S(1)} collective-permute-done((bf16[128,128]{1,0:T(8,128)(2,1)S(1)}, bf16[128,128]{1,0:T(8,128)(2,1)S(1)}, u32[]{:S(2)}, u32[]{:S(2)}) %collective-permute-start) | collective-permute-done | bytes 32800 | tf_op jit(solution)/shard_map/while/body/eval_jaxpr/ppermute | solution.py:12
  120.2 2.4 collective-permute-done.2
  126.3 3.1 %collective-permute-done = bf16[128,128]{1,0:T(8,128)(2,1)S(1)} collective-permute-done((bf16[128,128]{1,0:T(8,128)(2,1)S(1)}, bf16[128,128]{1,0:T(8,128)(2,1)S(1)}, u32[]{:S(2)}, u32[]{:S(2)}) %collective-permute-start) | collective-permute-done | bytes 32800 | tf_op jit(solution)/shard_map/while/body/eval_jaxpr/ppermute | solution.py:12
  129.8 2.4 collective-permute-done.2
  135.9 3.1 %collective-permute-done = bf16[128,128]{1,0:T(8,128)(2,1)S(1)} collective-permute-done((bf16[128,128]{1,0:T(8,128)(2,1)S(1)}, bf16[128,128]{1,0:T(8,128)(2,1)S(1)}, u32[]{:S(2)}, u32[]{:S(2)}) %collective-permute-start) | collective-permute-done | bytes 32800 | tf_op jit(solution)/shard_map/while/body/eval_jaxpr/ppermute | solution.py:12
  139.3 2.4 collective-permute-done.2
  145.4 3.1 %collective-permute-done = bf16[128,128]{1,0:T(8,128)(2,1)S(1)} collective-permute-done((bf16[128,128]{1,0:T(8,128)(2,1)S(1)}, bf16[128,128]{1,0:T(8,128)(2,1)S(1)}, u32[]{:S(2)}, u32[]{:S(2)}) %collective-permute-start) | collective-permute-done | bytes 32800 | tf_op jit(solution)/shard_map/while/body/eval_jaxpr/ppermute | solution.py:12
  148.8 2.4 collective-permute-done.2
  154.9 3.1 %collective-permute-done = bf16[128,128]{1,0:T(8,128)(2,1)S(1)} collective-permute-done((bf16[128,128]{1,0:T(8,128)(2,1)S(1)}, bf16[128,128]{1,0:T(8,128)(2,1)S(1)}, u32[]{:S(2)}, u32[]{:S(2)}) %collective-permute-start) | collective-permute-done | bytes 32800 | tf_op jit(solution)/shard_map/while/body/eval_jaxpr/ppermute | solution.py:12
  158.4 2.4 collective-permute-done.2
  164.5 3.1 %collective-permute-done = bf16[128,128]{1,0:T(8,128)(2,1)S(1)} collective-permute-done((bf16[128,128]{1,0:T(8,128)(2,1)S(1)}, bf16[128,128]{1,0:T(8,128)(2,1)S(1)}, u32[]{:S(2)}, u32[]{:S(2)}) %collective-permute-start) | collective-permute-done | bytes 32800 | tf_op jit(solution)/shard_map/while/body/eval_jaxpr/ppermute | solution.py:12
  167.9 2.4 collective-permute-done.2
  174.0 3.1 %collective-permute-done = bf16[128,128]{1,0:T(8,128)(2,1)S(1)} collective-permute-done((bf16[128,128]{1,0:T(8,128)(2,1)S(1)}, bf16[128,128]{1,0:T(8,128)(2,1)S(1)}, u32[]{:S(2)}, u32[]{:S(2)}) %collective-permute-start) | collective-permute-done | bytes 32800 | tf_op jit(solution)/shard_map/while/body/eval_jaxpr/ppermute | solution.py:12
  177.4 2.4 collective-permute-done.2
  183.5 3.1 %collective-permute-done = bf16[128,128]{1,0:T(8,128)(2,1)S(1)} collective-permute-done((bf16[128,128]{1,0:T(8,128)(2,1)S(1)}, bf16[128,128]{1,0:T(8,128)(2,1)S(1)}, u32[]{:S(2)}, u32[]{:S(2)}) %collective-permute-start) | collective-permute-done | bytes 32800 | tf_op jit(solution)/shard_map/while/body/eval_jaxpr/ppermute | solution.py:12
  186.9 2.4 collective-permute-done.2
  193.1 3.1 %collective-permute-done = bf16[128,128]{1,0:T(8,128)(2,1)S(1)} collective-permute-done((bf16[128,128]{1,0:T(8,128)(2,1)S(1)}, bf16[128,128]{1,0:T(8,128)(2,1)S(1)}, u32[]{:S(2)}, u32[]{:S(2)}) %collective-permute-start) | collective-permute-done | bytes 32800 | tf_op jit(solution)/shard_map/while/body/eval_jaxpr/ppermute | solution.py:12
  196.5 2.4 collective-permute-done.2
  202.6 3.1 %collective-permute-done = bf16[128,128]{1,0:T(8,128)(2,1)S(1)} collective-permute-done((bf16[128,128]{1,0:T(8,128)(2,1)S(1)}, bf16[128,128]{1,0:T(8,128)(2,1)S(1)}, u32[]{:S(2)}, u32[]{:S(2)}) %collective-permute-start) | collective-permute-done | bytes 32800 | tf_op jit(solution)/shard_map/while/body/eval_jaxpr/ppermute | solution.py:12
  206.0 2.4 collective-permute-done.2
  212.1 3.1 %collective-permute-done = bf16[128,128]{1,0:T(8,128)(2,1)S(1)} collective-permute-done((bf16[128,128]{1,0:T(8,128)(2,1)S(1)}, bf16[128,128]{1,0:T(8,128)(2,1)S(1)}, u32[]{:S(2)}, u32[]{:S(2)}) %collective-permute-start) | collective-permute-done | bytes 32800 | tf_op jit(solution)/shard_map/while/body/eval_jaxpr/ppermute | solution.py:12
  215.5 2.4 collective-permute-done.2
  221.7 3.1 %collective-permute-done = bf16[128,128]{1,0:T(8,128)(2,1)S(1)} collective-permute-done((bf16[128,128]{1,0:T(8,128)(2,1)S(1)}, bf16[128,128]{1,0:T(8,128)(2,1)S(1)}, u32[]{:S(2)}, u32[]{:S(2)}) %collective-permute-start) | collective-permute-done | bytes 32800 | tf_op jit(solution)/shard_map/while/body/eval_jaxpr/ppermute | solution.py:12
  225.1 2.4 collective-permute-done.2
  231.2 3.1 %collective-permute-done = bf16[128,128]{1,0:T(8,128)(2,1)S(1)} collective-permute-done((bf16[128,128]{1,0:T(8,128)(2,1)S(1)}, bf16[128,128]{1,0:T(8,128)(2,1)S(1)}, u32[]{:S(2)}, u32[]{:S(2)}) %collective-permute-start) | collective-permute-done | bytes 32800 | tf_op jit(solution)/shard_map/while/body/eval_jaxpr/ppermute | solution.py:12
  234.6 2.4 collective-permute-done.2
  240.4 4.2 %collective-permute-done.20 = f32[128,128]{1,0:T(8,128)S(1)} collective-permute-done((f32[128,128]{1,0:T(8,128)S(1)}, f32[128,128]{1,0:T(8,128)S(1)}, u32[]{:S(2)}, u32[]{:S(2)}) %collective-permute-start.20) | collective-permute-done | bytes 65568 | tf_op jit(solution)/shard_map/ppermute | solution.py:12
  (551 shorter events, 74.9 us)
Async XLA Ops:
  1.5 33.0 %collective-permute-start.4 = (bf16[128,128]{1,0:T(8,128)(2,1)S(1)}, bf16[128,128]{1,0:T(8,128)(2,1)S(1)}, u32[]{:S(2)}, u32[]{:S(2)}) collective-permute-start(bf16[128,128]{1,0:T(8,128)(2,1)S(1)} %copy.100), channel_id=1, source_target_pairs={{0,1},{1,2},{2,3},{3,4},{4,5},{5,6},{6,7},{7,8},{8,9},{9,10},{10,1... | collective-permute-start | bytes 98312 | tf_op jit(solution)/shard_map/ppermute | solution.py:94
  1.9 32.9 %collective-permute-start.5 = (bf16[128,128]{1,0:T(8,128)(2,1)S(1)}, bf16[128,128]{1,0:T(8,128)(2,1)S(1)}, u32[]{:S(2)}, u32[]{:S(2)}) collective-permute-start(bf16[128,128]{1,0:T(8,128)(2,1)S(1)} %copy.100), channel_id=1, source_target_pairs={{0,15},{1,0},{2,1},{3,2},{4,3},{5,4},{6,5},{7,6},{8,7},{9,8},{10,9... | collective-permute-start | bytes 98312 | tf_op jit(solution)/shard_map/ppermute | solution.py:101
  97.2 6.4 %collective-permute-start.2 = (f32[128,128]{1,0:T(8,128)S(1)}, f32[128,128]{1,0:T(8,128)S(1)}, u32[]{:S(2)}, u32[]{:S(2)}) collective-permute-start(f32[128,128]{1,0:T(8,128)S(1)} %fusion.123), channel_id=1, source_target_pairs={{0,1},{1,2},{2,3},{3,4},{4,5},{5,6},{6,7},{7,8},{8,9},{9,10},{10,1... | collective-permute-start | bytes 196616 | tf_op jit(solution)/shard_map/while/body/eval_jaxpr/ppermute | solution.py:12
  97.5 6.8 %collective-permute-start.3 = (f32[128,128]{1,0:T(8,128)S(1)}, f32[128,128]{1,0:T(8,128)S(1)}, u32[]{:S(2)}, u32[]{:S(2)}) collective-permute-start(f32[128,128]{1,0:T(8,128)S(1)} %convolution_add_fusion.6), channel_id=1, source_target_pairs={{0,1},{1,2},{2,3},{3,4},{4,5},{5,6},{6,7},{7,8},{8,9},{9,10},{10,1... | collective-permute-start | bytes 196616 | tf_op jit(solution)/shard_map/while/body/eval_jaxpr/ppermute | solution.py:12
  104.3 6.4 %collective-permute-start.1 = (bf16[128,128]{1,0:T(8,128)(2,1)S(1)}, bf16[128,128]{1,0:T(8,128)(2,1)S(1)}, u32[]{:S(2)}, u32[]{:S(2)}) collective-permute-start(bf16[128,128]{1,0:T(8,128)(2,1)S(1)} %copy.84), channel_id=1, source_target_pairs={{0,1},{1,2},{2,3},{3,4},{4,5},{5,6},{6,7},{7,8},{8,9},{9,10},{10,1... | collective-permute-start | bytes 98312 | tf_op jit(solution)/shard_map/while/body/eval_jaxpr/ppermute | solution.py:12
  106.7 6.4 %collective-permute-start.2 = (f32[128,128]{1,0:T(8,128)S(1)}, f32[128,128]{1,0:T(8,128)S(1)}, u32[]{:S(2)}, u32[]{:S(2)}) collective-permute-start(f32[128,128]{1,0:T(8,128)S(1)} %fusion.123), channel_id=1, source_target_pairs={{0,1},{1,2},{2,3},{3,4},{4,5},{5,6},{6,7},{7,8},{8,9},{9,10},{10,1... | collective-permute-start | bytes 196616 | tf_op jit(solution)/shard_map/while/body/eval_jaxpr/ppermute | solution.py:12
  107.0 6.8 %collective-permute-start.3 = (f32[128,128]{1,0:T(8,128)S(1)}, f32[128,128]{1,0:T(8,128)S(1)}, u32[]{:S(2)}, u32[]{:S(2)}) collective-permute-start(f32[128,128]{1,0:T(8,128)S(1)} %convolution_add_fusion.6), channel_id=1, source_target_pairs={{0,1},{1,2},{2,3},{3,4},{4,5},{5,6},{6,7},{7,8},{8,9},{9,10},{10,1... | collective-permute-start | bytes 196616 | tf_op jit(solution)/shard_map/while/body/eval_jaxpr/ppermute | solution.py:12
  113.8 6.4 %collective-permute-start.1 = (bf16[128,128]{1,0:T(8,128)(2,1)S(1)}, bf16[128,128]{1,0:T(8,128)(2,1)S(1)}, u32[]{:S(2)}, u32[]{:S(2)}) collective-permute-start(bf16[128,128]{1,0:T(8,128)(2,1)S(1)} %copy.84), channel_id=1, source_target_pairs={{0,1},{1,2},{2,3},{3,4},{4,5},{5,6},{6,7},{7,8},{8,9},{9,10},{10,1... | collective-permute-start | bytes 98312 | tf_op jit(solution)/shard_map/while/body/eval_jaxpr/ppermute | solution.py:12
  116.2 6.4 %collective-permute-start.2 = (f32[128,128]{1,0:T(8,128)S(1)}, f32[128,128]{1,0:T(8,128)S(1)}, u32[]{:S(2)}, u32[]{:S(2)}) collective-permute-start(f32[128,128]{1,0:T(8,128)S(1)} %fusion.123), channel_id=1, source_target_pairs={{0,1},{1,2},{2,3},{3,4},{4,5},{5,6},{6,7},{7,8},{8,9},{9,10},{10,1... | collective-permute-start | bytes 196616 | tf_op jit(solution)/shard_map/while/body/eval_jaxpr/ppermute | solution.py:12
  116.5 6.8 %collective-permute-start.3 = (f32[128,128]{1,0:T(8,128)S(1)}, f32[128,128]{1,0:T(8,128)S(1)}, u32[]{:S(2)}, u32[]{:S(2)}) collective-permute-start(f32[128,128]{1,0:T(8,128)S(1)} %convolution_add_fusion.6), channel_id=1, source_target_pairs={{0,1},{1,2},{2,3},{3,4},{4,5},{5,6},{6,7},{7,8},{8,9},{9,10},{10,1... | collective-permute-start | bytes 196616 | tf_op jit(solution)/shard_map/while/body/eval_jaxpr/ppermute | solution.py:12
  123.4 6.4 %collective-permute-start.1 = (bf16[128,128]{1,0:T(8,128)(2,1)S(1)}, bf16[128,128]{1,0:T(8,128)(2,1)S(1)}, u32[]{:S(2)}, u32[]{:S(2)}) collective-permute-start(bf16[128,128]{1,0:T(8,128)(2,1)S(1)} %copy.84), channel_id=1, source_target_pairs={{0,1},{1,2},{2,3},{3,4},{4,5},{5,6},{6,7},{7,8},{8,9},{9,10},{10,1... | collective-permute-start | bytes 98312 | tf_op jit(solution)/shard_map/while/body/eval_jaxpr/ppermute | solution.py:12
  125.8 6.4 %collective-permute-start.2 = (f32[128,128]{1,0:T(8,128)S(1)}, f32[128,128]{1,0:T(8,128)S(1)}, u32[]{:S(2)}, u32[]{:S(2)}) collective-permute-start(f32[128,128]{1,0:T(8,128)S(1)} %fusion.123), channel_id=1, source_target_pairs={{0,1},{1,2},{2,3},{3,4},{4,5},{5,6},{6,7},{7,8},{8,9},{9,10},{10,1... | collective-permute-start | bytes 196616 | tf_op jit(solution)/shard_map/while/body/eval_jaxpr/ppermute | solution.py:12
  126.1 6.8 %collective-permute-start.3 = (f32[128,128]{1,0:T(8,128)S(1)}, f32[128,128]{1,0:T(8,128)S(1)}, u32[]{:S(2)}, u32[]{:S(2)}) collective-permute-start(f32[128,128]{1,0:T(8,128)S(1)} %convolution_add_fusion.6), channel_id=1, source_target_pairs={{0,1},{1,2},{2,3},{3,4},{4,5},{5,6},{6,7},{7,8},{8,9},{9,10},{10,1... | collective-permute-start | bytes 196616 | tf_op jit(solution)/shard_map/while/body/eval_jaxpr/ppermute | solution.py:12
  132.9 6.4 %collective-permute-start.1 = (bf16[128,128]{1,0:T(8,128)(2,1)S(1)}, bf16[128,128]{1,0:T(8,128)(2,1)S(1)}, u32[]{:S(2)}, u32[]{:S(2)}) collective-permute-start(bf16[128,128]{1,0:T(8,128)(2,1)S(1)} %copy.84), channel_id=1, source_target_pairs={{0,1},{1,2},{2,3},{3,4},{4,5},{5,6},{6,7},{7,8},{8,9},{9,10},{10,1... | collective-permute-start | bytes 98312 | tf_op jit(solution)/shard_map/while/body/eval_jaxpr/ppermute | solution.py:12
  135.3 6.4 %collective-permute-start.2 = (f32[128,128]{1,0:T(8,128)S(1)}, f32[128,128]{1,0:T(8,128)S(1)}, u32[]{:S(2)}, u32[]{:S(2)}) collective-permute-start(f32[128,128]{1,0:T(8,128)S(1)} %fusion.123), channel_id=1, source_target_pairs={{0,1},{1,2},{2,3},{3,4},{4,5},{5,6},{6,7},{7,8},{8,9},{9,10},{10,1... | collective-permute-start | bytes 196616 | tf_op jit(solution)/shard_map/while/body/eval_jaxpr/ppermute | solution.py:12
  135.6 6.8 %collective-permute-start.3 = (f32[128,128]{1,0:T(8,128)S(1)}, f32[128,128]{1,0:T(8,128)S(1)}, u32[]{:S(2)}, u32[]{:S(2)}) collective-permute-start(f32[128,128]{1,0:T(8,128)S(1)} %convolution_add_fusion.6), channel_id=1, source_target_pairs={{0,1},{1,2},{2,3},{3,4},{4,5},{5,6},{6,7},{7,8},{8,9},{9,10},{10,1... | collective-permute-start | bytes 196616 | tf_op jit(solution)/shard_map/while/body/eval_jaxpr/ppermute | solution.py:12
  142.4 6.4 %collective-permute-start.1 = (bf16[128,128]{1,0:T(8,128)(2,1)S(1)}, bf16[128,128]{1,0:T(8,128)(2,1)S(1)}, u32[]{:S(2)}, u32[]{:S(2)}) collective-permute-start(bf16[128,128]{1,0:T(8,128)(2,1)S(1)} %copy.84), channel_id=1, source_target_pairs={{0,1},{1,2},{2,3},{3,4},{4,5},{5,6},{6,7},{7,8},{8,9},{9,10},{10,1... | collective-permute-start | bytes 98312 | tf_op jit(solution)/shard_map/while/body/eval_jaxpr/ppermute | solution.py:12
  144.8 6.4 %collective-permute-start.2 = (f32[128,128]{1,0:T(8,128)S(1)}, f32[128,128]{1,0:T(8,128)S(1)}, u32[]{:S(2)}, u32[]{:S(2)}) collective-permute-start(f32[128,128]{1,0:T(8,128)S(1)} %fusion.123), channel_id=1, source_target_pairs={{0,1},{1,2},{2,3},{3,4},{4,5},{5,6},{6,7},{7,8},{8,9},{9,10},{10,1... | collective-permute-start | bytes 196616 | tf_op jit(solution)/shard_map/while/body/eval_jaxpr/ppermute | solution.py:12
  145.1 6.8 %collective-permute-start.3 = (f32[128,128]{1,0:T(8,128)S(1)}, f32[128,128]{1,0:T(8,128)S(1)}, u32[]{:S(2)}, u32[]{:S(2)}) collective-permute-start(f32[128,128]{1,0:T(8,128)S(1)} %convolution_add_fusion.6), channel_id=1, source_target_pairs={{0,1},{1,2},{2,3},{3,4},{4,5},{5,6},{6,7},{7,8},{8,9},{9,10},{10,1... | collective-permute-start | bytes 196616 | tf_op jit(solution)/shard_map/while/body/eval_jaxpr/ppermute | solution.py:12
  152.0 6.4 %collective-permute-start.1 = (bf16[128,128]{1,0:T(8,128)(2,1)S(1)}, bf16[128,128]{1,0:T(8,128)(2,1)S(1)}, u32[]{:S(2)}, u32[]{:S(2)}) collective-permute-start(bf16[128,128]{1,0:T(8,128)(2,1)S(1)} %copy.84), channel_id=1, source_target_pairs={{0,1},{1,2},{2,3},{3,4},{4,5},{5,6},{6,7},{7,8},{8,9},{9,10},{10,1... | collective-permute-start | bytes 98312 | tf_op jit(solution)/shard_map/while/body/eval_jaxpr/ppermute | solution.py:12
  154.3 6.4 %collective-permute-start.2 = (f32[128,128]{1,0:T(8,128)S(1)}, f32[128,128]{1,0:T(8,128)S(1)}, u32[]{:S(2)}, u32[]{:S(2)}) collective-permute-start(f32[128,128]{1,0:T(8,128)S(1)} %fusion.123), channel_id=1, source_target_pairs={{0,1},{1,2},{2,3},{3,4},{4,5},{5,6},{6,7},{7,8},{8,9},{9,10},{10,1... | collective-permute-start | bytes 196616 | tf_op jit(solution)/shard_map/while/body/eval_jaxpr/ppermute | solution.py:12
  154.7 6.8 %collective-permute-start.3 = (f32[128,128]{1,0:T(8,128)S(1)}, f32[128,128]{1,0:T(8,128)S(1)}, u32[]{:S(2)}, u32[]{:S(2)}) collective-permute-start(f32[128,128]{1,0:T(8,128)S(1)} %convolution_add_fusion.6), channel_id=1, source_target_pairs={{0,1},{1,2},{2,3},{3,4},{4,5},{5,6},{6,7},{7,8},{8,9},{9,10},{10,1... | collective-permute-start | bytes 196616 | tf_op jit(solution)/shard_map/while/body/eval_jaxpr/ppermute | solution.py:12
  161.5 6.4 %collective-permute-start.1 = (bf16[128,128]{1,0:T(8,128)(2,1)S(1)}, bf16[128,128]{1,0:T(8,128)(2,1)S(1)}, u32[]{:S(2)}, u32[]{:S(2)}) collective-permute-start(bf16[128,128]{1,0:T(8,128)(2,1)S(1)} %copy.84), channel_id=1, source_target_pairs={{0,1},{1,2},{2,3},{3,4},{4,5},{5,6},{6,7},{7,8},{8,9},{9,10},{10,1... | collective-permute-start | bytes 98312 | tf_op jit(solution)/shard_map/while/body/eval_jaxpr/ppermute | solution.py:12
  163.9 6.4 %collective-permute-start.2 = (f32[128,128]{1,0:T(8,128)S(1)}, f32[128,128]{1,0:T(8,128)S(1)}, u32[]{:S(2)}, u32[]{:S(2)}) collective-permute-start(f32[128,128]{1,0:T(8,128)S(1)} %fusion.123), channel_id=1, source_target_pairs={{0,1},{1,2},{2,3},{3,4},{4,5},{5,6},{6,7},{7,8},{8,9},{9,10},{10,1... | collective-permute-start | bytes 196616 | tf_op jit(solution)/shard_map/while/body/eval_jaxpr/ppermute | solution.py:12
  164.2 6.8 %collective-permute-start.3 = (f32[128,128]{1,0:T(8,128)S(1)}, f32[128,128]{1,0:T(8,128)S(1)}, u32[]{:S(2)}, u32[]{:S(2)}) collective-permute-start(f32[128,128]{1,0:T(8,128)S(1)} %convolution_add_fusion.6), channel_id=1, source_target_pairs={{0,1},{1,2},{2,3},{3,4},{4,5},{5,6},{6,7},{7,8},{8,9},{9,10},{10,1... | collective-permute-start | bytes 196616 | tf_op jit(solution)/shard_map/while/body/eval_jaxpr/ppermute | solution.py:12
  171.0 6.4 %collective-permute-start.1 = (bf16[128,128]{1,0:T(8,128)(2,1)S(1)}, bf16[128,128]{1,0:T(8,128)(2,1)S(1)}, u32[]{:S(2)}, u32[]{:S(2)}) collective-permute-start(bf16[128,128]{1,0:T(8,128)(2,1)S(1)} %copy.84), channel_id=1, source_target_pairs={{0,1},{1,2},{2,3},{3,4},{4,5},{5,6},{6,7},{7,8},{8,9},{9,10},{10,1... | collective-permute-start | bytes 98312 | tf_op jit(solution)/shard_map/while/body/eval_jaxpr/ppermute | solution.py:12
  173.4 6.4 %collective-permute-start.2 = (f32[128,128]{1,0:T(8,128)S(1)}, f32[128,128]{1,0:T(8,128)S(1)}, u32[]{:S(2)}, u32[]{:S(2)}) collective-permute-start(f32[128,128]{1,0:T(8,128)S(1)} %fusion.123), channel_id=1, source_target_pairs={{0,1},{1,2},{2,3},{3,4},{4,5},{5,6},{6,7},{7,8},{8,9},{9,10},{10,1... | collective-permute-start | bytes 196616 | tf_op jit(solution)/shard_map/while/body/eval_jaxpr/ppermute | solution.py:12
  173.7 6.8 %collective-permute-start.3 = (f32[128,128]{1,0:T(8,128)S(1)}, f32[128,128]{1,0:T(8,128)S(1)}, u32[]{:S(2)}, u32[]{:S(2)}) collective-permute-start(f32[128,128]{1,0:T(8,128)S(1)} %convolution_add_fusion.6), channel_id=1, source_target_pairs={{0,1},{1,2},{2,3},{3,4},{4,5},{5,6},{6,7},{7,8},{8,9},{9,10},{10,1... | collective-permute-start | bytes 196616 | tf_op jit(solution)/shard_map/while/body/eval_jaxpr/ppermute | solution.py:12
  180.6 6.4 %collective-permute-start.1 = (bf16[128,128]{1,0:T(8,128)(2,1)S(1)}, bf16[128,128]{1,0:T(8,128)(2,1)S(1)}, u32[]{:S(2)}, u32[]{:S(2)}) collective-permute-start(bf16[128,128]{1,0:T(8,128)(2,1)S(1)} %copy.84), channel_id=1, source_target_pairs={{0,1},{1,2},{2,3},{3,4},{4,5},{5,6},{6,7},{7,8},{8,9},{9,10},{10,1... | collective-permute-start | bytes 98312 | tf_op jit(solution)/shard_map/while/body/eval_jaxpr/ppermute | solution.py:12
  182.9 6.4 %collective-permute-start.2 = (f32[128,128]{1,0:T(8,128)S(1)}, f32[128,128]{1,0:T(8,128)S(1)}, u32[]{:S(2)}, u32[]{:S(2)}) collective-permute-start(f32[128,128]{1,0:T(8,128)S(1)} %fusion.123), channel_id=1, source_target_pairs={{0,1},{1,2},{2,3},{3,4},{4,5},{5,6},{6,7},{7,8},{8,9},{9,10},{10,1... | collective-permute-start | bytes 196616 | tf_op jit(solution)/shard_map/while/body/eval_jaxpr/ppermute | solution.py:12
  183.2 6.8 %collective-permute-start.3 = (f32[128,128]{1,0:T(8,128)S(1)}, f32[128,128]{1,0:T(8,128)S(1)}, u32[]{:S(2)}, u32[]{:S(2)}) collective-permute-start(f32[128,128]{1,0:T(8,128)S(1)} %convolution_add_fusion.6), channel_id=1, source_target_pairs={{0,1},{1,2},{2,3},{3,4},{4,5},{5,6},{6,7},{7,8},{8,9},{9,10},{10,1... | collective-permute-start | bytes 196616 | tf_op jit(solution)/shard_map/while/body/eval_jaxpr/ppermute | solution.py:12
  190.1 6.4 %collective-permute-start.1 = (bf16[128,128]{1,0:T(8,128)(2,1)S(1)}, bf16[128,128]{1,0:T(8,128)(2,1)S(1)}, u32[]{:S(2)}, u32[]{:S(2)}) collective-permute-start(bf16[128,128]{1,0:T(8,128)(2,1)S(1)} %copy.84), channel_id=1, source_target_pairs={{0,1},{1,2},{2,3},{3,4},{4,5},{5,6},{6,7},{7,8},{8,9},{9,10},{10,1... | collective-permute-start | bytes 98312 | tf_op jit(solution)/shard_map/while/body/eval_jaxpr/ppermute | solution.py:12
  192.5 6.4 %collective-permute-start.2 = (f32[128,128]{1,0:T(8,128)S(1)}, f32[128,128]{1,0:T(8,128)S(1)}, u32[]{:S(2)}, u32[]{:S(2)}) collective-permute-start(f32[128,128]{1,0:T(8,128)S(1)} %fusion.123), channel_id=1, source_target_pairs={{0,1},{1,2},{2,3},{3,4},{4,5},{5,6},{6,7},{7,8},{8,9},{9,10},{10,1... | collective-permute-start | bytes 196616 | tf_op jit(solution)/shard_map/while/body/eval_jaxpr/ppermute | solution.py:12
  192.8 6.8 %collective-permute-start.3 = (f32[128,128]{1,0:T(8,128)S(1)}, f32[128,128]{1,0:T(8,128)S(1)}, u32[]{:S(2)}, u32[]{:S(2)}) collective-permute-start(f32[128,128]{1,0:T(8,128)S(1)} %convolution_add_fusion.6), channel_id=1, source_target_pairs={{0,1},{1,2},{2,3},{3,4},{4,5},{5,6},{6,7},{7,8},{8,9},{9,10},{10,1... | collective-permute-start | bytes 196616 | tf_op jit(solution)/shard_map/while/body/eval_jaxpr/ppermute | solution.py:12
  199.6 6.4 %collective-permute-start.1 = (bf16[128,128]{1,0:T(8,128)(2,1)S(1)}, bf16[128,128]{1,0:T(8,128)(2,1)S(1)}, u32[]{:S(2)}, u32[]{:S(2)}) collective-permute-start(bf16[128,128]{1,0:T(8,128)(2,1)S(1)} %copy.84), channel_id=1, source_target_pairs={{0,1},{1,2},{2,3},{3,4},{4,5},{5,6},{6,7},{7,8},{8,9},{9,10},{10,1... | collective-permute-start | bytes 98312 | tf_op jit(solution)/shard_map/while/body/eval_jaxpr/ppermute | solution.py:12
  202.0 6.4 %collective-permute-start.2 = (f32[128,128]{1,0:T(8,128)S(1)}, f32[128,128]{1,0:T(8,128)S(1)}, u32[]{:S(2)}, u32[]{:S(2)}) collective-permute-start(f32[128,128]{1,0:T(8,128)S(1)} %fusion.123), channel_id=1, source_target_pairs={{0,1},{1,2},{2,3},{3,4},{4,5},{5,6},{6,7},{7,8},{8,9},{9,10},{10,1... | collective-permute-start | bytes 196616 | tf_op jit(solution)/shard_map/while/body/eval_jaxpr/ppermute | solution.py:12
  202.3 6.8 %collective-permute-start.3 = (f32[128,128]{1,0:T(8,128)S(1)}, f32[128,128]{1,0:T(8,128)S(1)}, u32[]{:S(2)}, u32[]{:S(2)}) collective-permute-start(f32[128,128]{1,0:T(8,128)S(1)} %convolution_add_fusion.6), channel_id=1, source_target_pairs={{0,1},{1,2},{2,3},{3,4},{4,5},{5,6},{6,7},{7,8},{8,9},{9,10},{10,1... | collective-permute-start | bytes 196616 | tf_op jit(solution)/shard_map/while/body/eval_jaxpr/ppermute | solution.py:12
  209.2 6.4 %collective-permute-start.1 = (bf16[128,128]{1,0:T(8,128)(2,1)S(1)}, bf16[128,128]{1,0:T(8,128)(2,1)S(1)}, u32[]{:S(2)}, u32[]{:S(2)}) collective-permute-start(bf16[128,128]{1,0:T(8,128)(2,1)S(1)} %copy.84), channel_id=1, source_target_pairs={{0,1},{1,2},{2,3},{3,4},{4,5},{5,6},{6,7},{7,8},{8,9},{9,10},{10,1... | collective-permute-start | bytes 98312 | tf_op jit(solution)/shard_map/while/body/eval_jaxpr/ppermute | solution.py:12
  211.5 6.4 %collective-permute-start.2 = (f32[128,128]{1,0:T(8,128)S(1)}, f32[128,128]{1,0:T(8,128)S(1)}, u32[]{:S(2)}, u32[]{:S(2)}) collective-permute-start(f32[128,128]{1,0:T(8,128)S(1)} %fusion.123), channel_id=1, source_target_pairs={{0,1},{1,2},{2,3},{3,4},{4,5},{5,6},{6,7},{7,8},{8,9},{9,10},{10,1... | collective-permute-start | bytes 196616 | tf_op jit(solution)/shard_map/while/body/eval_jaxpr/ppermute | solution.py:12
  211.8 6.8 %collective-permute-start.3 = (f32[128,128]{1,0:T(8,128)S(1)}, f32[128,128]{1,0:T(8,128)S(1)}, u32[]{:S(2)}, u32[]{:S(2)}) collective-permute-start(f32[128,128]{1,0:T(8,128)S(1)} %convolution_add_fusion.6), channel_id=1, source_target_pairs={{0,1},{1,2},{2,3},{3,4},{4,5},{5,6},{6,7},{7,8},{8,9},{9,10},{10,1... | collective-permute-start | bytes 196616 | tf_op jit(solution)/shard_map/while/body/eval_jaxpr/ppermute | solution.py:12
  218.7 6.4 %collective-permute-start.1 = (bf16[128,128]{1,0:T(8,128)(2,1)S(1)}, bf16[128,128]{1,0:T(8,128)(2,1)S(1)}, u32[]{:S(2)}, u32[]{:S(2)}) collective-permute-start(bf16[128,128]{1,0:T(8,128)(2,1)S(1)} %copy.84), channel_id=1, source_target_pairs={{0,1},{1,2},{2,3},{3,4},{4,5},{5,6},{6,7},{7,8},{8,9},{9,10},{10,1... | collective-permute-start | bytes 98312 | tf_op jit(solution)/shard_map/while/body/eval_jaxpr/ppermute | solution.py:12
  221.1 6.4 %collective-permute-start.2 = (f32[128,128]{1,0:T(8,128)S(1)}, f32[128,128]{1,0:T(8,128)S(1)}, u32[]{:S(2)}, u32[]{:S(2)}) collective-permute-start(f32[128,128]{1,0:T(8,128)S(1)} %fusion.123), channel_id=1, source_target_pairs={{0,1},{1,2},{2,3},{3,4},{4,5},{5,6},{6,7},{7,8},{8,9},{9,10},{10,1... | collective-permute-start | bytes 196616 | tf_op jit(solution)/shard_map/while/body/eval_jaxpr/ppermute | solution.py:12
  221.4 6.8 %collective-permute-start.3 = (f32[128,128]{1,0:T(8,128)S(1)}, f32[128,128]{1,0:T(8,128)S(1)}, u32[]{:S(2)}, u32[]{:S(2)}) collective-permute-start(f32[128,128]{1,0:T(8,128)S(1)} %convolution_add_fusion.6), channel_id=1, source_target_pairs={{0,1},{1,2},{2,3},{3,4},{4,5},{5,6},{6,7},{7,8},{8,9},{9,10},{10,1... | collective-permute-start | bytes 196616 | tf_op jit(solution)/shard_map/while/body/eval_jaxpr/ppermute | solution.py:12
  228.2 6.4 %collective-permute-start.1 = (bf16[128,128]{1,0:T(8,128)(2,1)S(1)}, bf16[128,128]{1,0:T(8,128)(2,1)S(1)}, u32[]{:S(2)}, u32[]{:S(2)}) collective-permute-start(bf16[128,128]{1,0:T(8,128)(2,1)S(1)} %copy.84), channel_id=1, source_target_pairs={{0,1},{1,2},{2,3},{3,4},{4,5},{5,6},{6,7},{7,8},{8,9},{9,10},{10,1... | collective-permute-start | bytes 98312 | tf_op jit(solution)/shard_map/while/body/eval_jaxpr/ppermute | solution.py:12
  230.6 6.4 %collective-permute-start.2 = (f32[128,128]{1,0:T(8,128)S(1)}, f32[128,128]{1,0:T(8,128)S(1)}, u32[]{:S(2)}, u32[]{:S(2)}) collective-permute-start(f32[128,128]{1,0:T(8,128)S(1)} %fusion.123), channel_id=1, source_target_pairs={{0,1},{1,2},{2,3},{3,4},{4,5},{5,6},{6,7},{7,8},{8,9},{9,10},{10,1... | collective-permute-start | bytes 196616 | tf_op jit(solution)/shard_map/while/body/eval_jaxpr/ppermute | solution.py:12
  230.9 6.8 %collective-permute-start.3 = (f32[128,128]{1,0:T(8,128)S(1)}, f32[128,128]{1,0:T(8,128)S(1)}, u32[]{:S(2)}, u32[]{:S(2)}) collective-permute-start(f32[128,128]{1,0:T(8,128)S(1)} %convolution_add_fusion.6), channel_id=1, source_target_pairs={{0,1},{1,2},{2,3},{3,4},{4,5},{5,6},{6,7},{7,8},{8,9},{9,10},{10,1... | collective-permute-start | bytes 196616 | tf_op jit(solution)/shard_map/while/body/eval_jaxpr/ppermute | solution.py:12
  238.2 6.4 %collective-permute-start.20 = (f32[128,128]{1,0:T(8,128)S(1)}, f32[128,128]{1,0:T(8,128)S(1)}, u32[]{:S(2)}, u32[]{:S(2)}) collective-permute-start(f32[128,128]{1,0:T(8,128)S(1)} %convolution_add_fusion.2), channel_id=1, source_target_pairs={{0,1},{1,2},{2,3},{3,4},{4,5},{5,6},{6,7},{7,8},{8,9},{9,10},{10,1... | collective-permute-start | bytes 196616 | tf_op jit(solution)/shard_map/ppermute | solution.py:12
  238.7 6.7 %collective-permute-start.19 = (f32[128,128]{1,0:T(8,128)S(1)}, f32[128,128]{1,0:T(8,128)S(1)}, u32[]{:S(2)}, u32[]{:S(2)}) collective-permute-start(f32[128,128]{1,0:T(8,128)S(1)} %fusion.45), channel_id=1, source_target_pairs={{0,1},{1,2},{2,3},{3,4},{4,5},{5,6},{6,7},{7,8},{8,9},{9,10},{10,1... | collective-permute-start | bytes 196616 | tf_op jit(solution)/shard_map/ppermute | solution.py:12
  (33 other events, 207.8 us)
